TPU v7x, 256 devices: a whole 4x4x8 slice. The times are simulated.
256 devices in a mesh: amp: 32 (over y, z), ints: 8 (over x, core).
Axes of the slice: x: 4, y: 4, z: 8, core: 2. Of those that a mesh axis runs over, the one named last changes fastest.
Arguments:
- amplitudes: bfloat16 [64, 1024, 1024], P('amp', None, 'ints'), may hold values from -6 to 6
- fock_vv: bfloat16 [1024, 1024], replicated, may hold values from -0.1875 to 0.1875
- cycle_ints: bfloat16 [4, 1024, 4, 1024], P(None, 'amp', None, 'ints'), may hold values from -0.15625 to 0.15625
- tile_mask: int32 [16, 16], replicated, may hold values 0 or 1
Outputs:
- residual: bfloat16 [64, 1024, 1024], P('amp', None, 'ints')
All inputs are finite; a program needn't handle non-finite values.
Results may differ from a plain program's by a relative error of at most 0.0034.
Values may be sent and summed in bfloat16 or wider, within the bound.
No kernel may reach another device: no remote copies, remote signals or barrier semaphores. Data moves between devices by JAX's collectives and lax.ppermute only.
A program may use at most 64 MiB of HBM per device.

v0:
```python
import jax
import jax.numpy as jnp
from jax import lax
from jax.sharding import PartitionSpec as P


def body(amplitudes, fock_vv, cycle_ints, tile_mask):
    n_amp = lax.axis_size("amp")
    ints_index = lax.axis_index("ints")
    pairs_dev, width, col_width = amplitudes.shape
    width_a = width // n_amp
    occ_k = cycle_ints.shape[0]
    occ_i = pairs_dev * n_amp // occ_k
    n_blocks = tile_mask.shape[0]
    block_size = width // n_blocks
    block_range = jnp.arange(n_blocks)
    row_select = ((jnp.arange(width) // block_size)[:, None] == block_range[None, :]).astype(
        jnp.float32
    )
    col_ids = (ints_index * col_width + jnp.arange(col_width)) // block_size
    col_select = (col_ids[:, None] == block_range[None, :]).astype(jnp.float32)
    expanded = jnp.dot(jnp.dot(row_select, tile_mask.astype(jnp.float32)), col_select.T)
    ints_full = lax.all_gather(cycle_ints, "amp", axis=1, tiled=True)
    masked = ints_full * expanded.astype(jnp.bfloat16)[None, :, None, :]
    left_term = jnp.einsum("ac,pcb->pab", fock_vv, amplitudes, preferred_element_type=jnp.float32)
    fock_rows = lax.dynamic_slice_in_dim(fock_vv, ints_index * col_width, col_width, 0)
    right_term = jnp.einsum(
        "pac,bc->pab",
        lax.all_gather(amplitudes, "ints", axis=2, tiled=True),
        fock_rows,
        preferred_element_type=jnp.float32,
    )
    virtual = lax.all_to_all(amplitudes, "amp", split_axis=1, concat_axis=0, tiled=True)
    shard_piece = lax.all_gather(virtual, "ints", axis=2, tiled=True)
    grouped = shard_piece.reshape(occ_i, occ_k, width_a, shard_piece.shape[2])
    cycle_term = jnp.einsum("ikac,kcjb->ijab", grouped, masked, preferred_element_type=jnp.float32)
    cycle_pairs = cycle_term.astype(jnp.bfloat16).reshape(occ_i * occ_k, width_a, col_width)
    returned = lax.all_to_all(cycle_pairs, "amp", split_axis=0, concat_axis=1, tiled=True)
    total = left_term + right_term + returned.astype(jnp.float32)
    return total.astype(jnp.bfloat16)


def solution(mesh):
    in_specs = (P("amp", None, "ints"), P(), P(None, "amp", None, "ints"), P())
    out_specs = P("amp", None, "ints")
    return jax.shard_map(body, mesh=mesh, in_specs=in_specs, out_specs=out_specs, check_vma=False)
```

profile of v0, /device:TPU:8, one launch (start us, length us, event | category | flops | bytes accessed | tf_op | source)
XLA Modules:
  0.0 187.8 jit_solution(17632588910587969167)
XLA Ops:
  6.5 0.0 copy-start
  6.5 0.0 copy-start.3
  6.5 0.0 all-gather.6.cloned.1.call-start
  6.5 0.7 all-gather.6.cloned.1.call-update
  7.3 0.0 all-gather.8.cloned.1.call-start
  7.3 1.6 copy.17
  8.9 28.6 %all_to_all.27 = bf16[2,1024,128]{2,0,1:T(2,128)(2,1)S(1)} all-to-all(bf16[2,1024,128]{2,0,1:T(2,128)(2,1)S(1)} %copy.17), channel_id=1, replica_groups=mesh['amp'=32,'ints'=8] {'amp'}, dimensions={1} | all-to-all | bytes 1048576 | tf_op jit(solution)/shard_map/all_to_all | solution.py:33
  37.5 0.9 copy.18
  38.4 0.0 all-gather.8.cloned.1.call-update
  38.4 0.0 all-gather.4.cloned.1.call-start
  38.4 0.7 all-gather.4.cloned.1.call-update
  39.2 0.0 copy-done.3
  39.2 0.6 convolution_convert_fusion
  39.7 54.2 %all-gather.6.cloned.1.call-done = bf16[4,1024,4,128]{3,2,1,0:T(4,128)(2,1)} async-done(((bf16[4,32,4,128]{3,2,1,0:T(4,128)(2,1)}), bf16[4,1024,4,128]{3,2,1,0:T(4,128)(2,1)}) %all-gather.6.cloned.1.call-update) | async-done | bytes 4194320 | tf_op jit(solution)/shard_map/all_gather | solution.py:23
  94.0 6.1 %multiply_bitcast_fusion = bf16[4,1024,4,128,1]{3,2,1,0,4:T(4,128)(2,1)} fusion(bf16[4,1024,4,128]{3,2,1,0:T(4,128)(2,1)} %all-gather.6.cloned.1.call-done, bf16[1024,128]{1,0:T(8,128)(2,1)S(1)} %convolution_convert_fusion), kind=kLoop, calls=%fused_computation.2 | loop fusion | flops 2097152 | bytes 8650752 | tf_op jit(solution)/shard_map/mul | solution.py:24
  100.0 32.9 %all-gather.8.cloned.1.call-done = bf16[64,32,1024]{2,1,0:T(8,128)(2,1)} async-done(((bf16[64,32,128]{2,1,0:T(8,128)(2,1)}), bf16[64,32,1024]{2,1,0:T(8,128)(2,1)}) %all-gather.8.cloned.1.call-update) | async-done | bytes 4194320 | tf_op jit(solution)/shard_map/all_gather | solution.py:34
  132.9 0.0 copy-start.1
  132.9 5.8 %fusion.16 = bf16[16,4,32,128]{3,2,0,1:T(8,128)(2,1)S(1)} fusion(bf16[16,4,32,1024,1]{3,2,1,0,4:T(8,128)(2,1)} %bitcast.48, bf16[4,1024,4,128,1]{3,2,1,0,4:T(4,128)(2,1)} %multiply_bitcast_fusion), kind=kOutput, calls=%fused_computation.12 | convolution fusion | flops 2147745792 | bytes 8912896 | tf_op jit(solution)/shard_map/ikac,kcjb->ijab/dot_general | solution.py:36
  138.8 0.9 copy.20
  139.6 10.2 %all-to-all-start.1 = ((bf16[64,32,128]{2,1,0:T(8,128)(2,1)}), bf16[64,32,128]{2,1,0:T(8,128)(2,1)}, u32[]{:S(2)}, u32[]{:S(2)}) async-start(bf16[64,32,128]{2,1,0:T(8,128)(2,1)} %bitcast.13), calls=%async_computation.1 | async-start | bytes 1048576 | tf_op jit(solution)/shard_map/all_to_all | solution.py:38
  149.8 0.0 copy-done
  149.8 0.0 copy-done.1
  149.8 1.8 fusion.4
  151.6 0.0 copy-start.2
  151.6 14.2 %all-to-all-done.1 = bf16[64,32,128]{2,1,0:T(8,128)(2,1)} async-done(((bf16[64,32,128]{2,1,0:T(8,128)(2,1)}), bf16[64,32,128]{2,1,0:T(8,128)(2,1)}, u32[]{:S(2)}, u32[]{:S(2)}) %all-to-all-start.1) | async-done | bytes 524320 | tf_op jit(solution)/shard_map/all_to_all | solution.py:38
  165.9 1.2 convert_bitcast_fusion
  167.0 1.1 copy.21
  168.1 2.5 %copy.22 = f32[2,1024,128]{1,2,0:T(8,128)} copy(f32[2,1024,128]{2,1,0:T(8,128)} %bitcast.45) | data formatting | bytes 2097152 | tf_op jit(solution)/shard_map/convert_element_type | solution.py:39
  170.7 3.7 %all-gather.4.cloned.1.call-done = bf16[2,1024,1024]{2,1,0:T(8,128)(2,1)} async-done(((bf16[2,1024,128]{2,1,0:T(8,128)(2,1)}), bf16[2,1024,1024]{2,1,0:T(8,128)(2,1)}) %all-gather.4.cloned.1.call-update) | async-done | bytes 4194320 | tf_op jit(solution)/shard_map/all_gather | solution.py:29
  174.4 0.0 copy-done.2
  174.4 4.8 %fusion.12 = bf16[2,1024,128]{1,2,0:T(8,128)(2,1)} fusion(f32[2,1024,128]{1,2,0:T(8,128)} %copy.22, f32[2,1024,128]{1,2,0:T(8,128)S(1)} %copy-done.2, bf16[2,1024,1024]{2,1,0:T(8,128)(2,1)} %all-gather.4.cloned.1.call-done, bf16[1024,1024]{1,0:T(8,128)(2,1)S(1)} %copy-done, s32[]{:T(128)S(6)} %select_n.21), kind=kOutput, calls=%fused_computation.10 | convolution fusion | flops 537657344 | bytes 7077892 | tf_op jit(solution)/shard_map/pac,bc->pab/dot_general | solution.py:27
  179.2 2.0 %copy.23 = bf16[2,1024,128]{2,1,0:T(8,128)(2,1)} copy(bf16[2,1024,128]{1,2,0:T(8,128)(2,1)} %fusion.12) | data formatting | bytes 1048576 | tf_op jit(solution)/shard_map/convert_element_type | solution.py:40
  (2 shorter events, 0.0 us)
Async XLA Ops:
  6.5 143.3 %copy-start = (bf16[1024,1024]{1,0:T(8,128)(2,1)S(1)}, bf16[1024,1024]{1,0:T(8,128)(2,1)}, u32[]{:S(2)}) copy-start(bf16[1024,1024]{1,0:T(8,128)(2,1)} %param.5) | copy-start | bytes 6291460
  6.5 32.6 %copy-start.3 = (s32[16,16]{1,0:T(8,128)S(1)}, s32[16,16]{1,0:T(8,128)}, u32[]{:S(2)}) copy-start(s32[16,16]{1,0:T(8,128)} %param.7) | copy-start | bytes 3076
  6.5 87.4 %all-gather.6.cloned.1.call-start = ((), (), s32[]{:S(2)}) async-start(), calls=%async_computation.3 | async-start | bytes 4325376 | tf_op jit(solution)/shard_map/all_gather | solution.py:23
  7.3 125.6 %all-gather.8.cloned.1.call-start = ((), (), s32[]{:S(2)}) async-start(), calls=%async_computation.4 | async-start | bytes 4718592 | tf_op jit(solution)/shard_map/all_gather | solution.py:34
  38.4 136.0 %all-gather.4.cloned.1.call-start = ((), (), s32[]{:S(2)}) async-start(), calls=%async_computation.2 | async-start | bytes 4718592 | tf_op jit(solution)/shard_map/all_gather | solution.py:29
  132.9 16.9 %copy-start.1 = (bf16[2,1024,128]{2,1,0:T(8,128)(2,1)S(1)}, bf16[2,1024,128]{2,1,0:T(8,128)(2,1)}, u32[]{:S(2)}) copy-start(bf16[2,1024,128]{2,1,0:T(8,128)(2,1)} %param.4) | copy-start | bytes 1572868
  139.6 26.3 %all-to-all-start.1 = ((bf16[64,32,128]{2,1,0:T(8,128)(2,1)}), bf16[64,32,128]{2,1,0:T(8,128)(2,1)}, u32[]{:S(2)}, u32[]{:S(2)}) async-start(bf16[64,32,128]{2,1,0:T(8,128)(2,1)} %bitcast.13), calls=%async_computation.1 | async-start | bytes 1048576 | tf_op jit(solution)/shard_map/all_to_all | solution.py:38
  151.6 22.8 %copy-start.2 = (f32[2,1024,128]{1,2,0:T(8,128)S(1)}, f32[2,1024,128]{1,2,0:T(8,128)}, u32[]{:S(2)}) copy-start(f32[2,1024,128]{1,2,0:T(8,128)} %fusion.4) | copy-start | bytes 3145732
Sparse Core Ops, SparseCore 0:
  10.0 83.9 all-gather.5
  95.8 37.0 all-gather.7
  134.7 39.5 all-gather.3
where the time goes:
time: 190 us; the launch traced here: 188 us
  waiting for transfers between devices  106 us (56%)
  blocking collectives  28.6 us (15%)
  between operations  13.2 us (7%)
  matrix products  13 us (7%)
  starting transfers between devices  10.3 us (5%)
  local copies, waits for them, and re-layouts  9.03 us (5%)
  other arithmetic  7.25 us (4%)
    all_gather x1, waiting for transfers between devices, body(): ints_full = lax.all_gather(cycle_ints, 'amp', axis=1, tiled=True)  54.2 us
    all_gather x1, waiting for transfers between devices, body(): shard_piece = lax.all_gather(virtual, 'ints', axis=2, tiled=True)  32.9 us
    all_to_all x1, blocking collectives, body(): lax.all_to_all(amplitudes, 'amp', split_axis=1, concat_axis=0, tiled=True)  28.6 us
    all_to_all x1, waiting for transfers between devices, body(): lax.all_to_all(cycle_pairs, 'amp', split_axis=0, concat_axis=1, tiled=True)  14.2 us
    all_to_all x1, starting transfers between devices, body(): lax.all_to_all(cycle_pairs, 'amp', split_axis=0, concat_axis=1, tiled=True)  10.2 us
    mul x1, other arithmetic, body(): masked = ints_full * expanded.astype(jnp.bfloat16)[None, :, None, :]  6.07 us
    dot_general x1, matrix products, body(): jnp.einsum('ikac,kcjb->ijab', grouped, masked, preferred_element_type=jnp...  5.84 us
    dot_general x1, matrix products, body(): jnp.einsum('pac,bc->pab', lax.all_gather(amplitudes, 'ints', axis=2, tile...  4.84 us
  transfers between devices with their start and end apart: 4, of which 4 were waited for; matrix products, arithmetic and copies ran while one was open for 12% of the time, Pallas kernels for 0%

commit v1 on v0

v1 whole, which is shorter than its diff:
```python
import jax
import jax.numpy as jnp
from jax import lax
from jax.experimental import pallas as pl
from jax.experimental.pallas import tpu as pltpu
from jax.sharding import PartitionSpec as P

NX, NY, NZ = 4, 4, 8
X_RING = lambda d: [(2 * x + c, 2 * ((x + d) % NX) + c) for x in range(NX) for c in range(2)]
Y_RING = lambda d: [(y * NZ + z, ((y + d) % NY) * NZ + z) for y in range(NY) for z in range(NZ)]
Z_PAIR = [(p, p ^ 1) for p in range(NY * NZ)]
CORES = [(q, q ^ 1) for q in range(2 * NX)]
Z_GROUPS = [[y * NZ + z for z in range(NZ)] for y in range(NY)]
ROWS = 256
MIB = 1 << 20


def fock_kernel(at_ref, fock_ref, rows_ref, amps_ref, *refs):
    mine, swapped, out_ref = refs[:NX], refs[NX : 2 * NX], refs[2 * NX]
    x, core = at_ref[2], at_ref[3]
    both = jnp.concatenate([amps_ref[0], amps_ref[1]], axis=1)
    left = jnp.dot(fock_ref[...], both, preferred_element_type=jnp.float32)
    width = amps_ref.shape[2]
    fock = []
    for d in range(NX):
        for c in (core, 1 - core):
            start = pl.multiple_of((2 * lax.rem(x + d, NX) + c) * width, width)
            fock.append(rows_ref[:, pl.ds(start, width)])
    fock = jnp.concatenate(fock, axis=1)
    for p in range(2):
        rows = jnp.concatenate([r[p] for d in range(NX) for r in (mine[d], swapped[d])], axis=1)
        right = lax.dot_general(
            rows, fock, (((1,), (1,)), ((), ())), preferred_element_type=jnp.float32
        )
        out_ref[p] = left[:, p * width : (p + 1) * width] + right


def fock_terms(at, fock_vv, amplitudes, mine, swapped):
    pairs, width, cols = amplitudes.shape
    block = pl.BlockSpec((pairs, ROWS, cols), lambda r, at: (0, r, 0))
    return pl.pallas_call(
        fock_kernel,
        out_shape=jax.ShapeDtypeStruct((pairs, width, cols), jnp.float32),
        grid_spec=pltpu.PrefetchScalarGridSpec(
            num_scalar_prefetch=1,
            grid=(width // ROWS,),
            in_specs=[
                pl.BlockSpec((ROWS, width), lambda r, at: (r, 0)),
                pl.BlockSpec((cols, width), lambda r, at: (2 * at[2] + at[3], 0)),
                pl.BlockSpec((pairs, width, cols), lambda r, at: (0, 0, 0)),
            ]
            + [block] * (2 * NX),
            out_specs=block,
        ),
        compiler_params=pltpu.CompilerParams(vmem_limit_bytes=24 * MIB),
        cost_estimate=pl.CostEstimate(
            flops=2 * pairs * width * width * cols * 2, bytes_accessed=9 * MIB, transcendentals=0
        ),
    )(at, fock_vv, fock_vv, amplitudes, *mine, *swapped)


def cycle_kernel(at_ref, fock_ref, *refs):
    amps, ints, out_ref, held = refs[: 4 * NX], refs[4 * NX : 4 * NX + NY], refs[-2], refs[-1]
    y, half, x, core = at_ref[0], lax.rem(at_ref[1], 2), at_ref[2], at_ref[3]

    @pl.when(pl.program_id(0) == 0)
    def _():
        for e in range(NY):
            held[lax.rem(y + e, NY)] = ints[e][...]

    n_z, _, depth, cols = ints[0].shape[0:4]
    side = n_z // 2
    total = None
    for d in range(NX):
        lhs, rhs = [], []
        for o in range(2):
            mine, swapped = amps[2 * NX * o + d], amps[2 * NX * o + NX + d]
            for p in range(2):
                k = 2 * (half if o == 0 else 1 - half) + p
                for ref, c in ((mine, core), (swapped, 1 - core)):
                    lhs.append(ref[p])
                    part = held[lax.rem(x + d, NX), pl.ds(c * side, side), k]
                    rhs.append(part.reshape(side * depth, cols))
        term = jnp.dot(
            jnp.concatenate(lhs, axis=1),
            jnp.concatenate(rhs, axis=0),
            preferred_element_type=jnp.float32,
        )
        total = term if total is None else total + term
    width = cols // 2
    total = total.astype(jnp.bfloat16).astype(jnp.float32)
    for p in range(2):
        out_ref[p] = (fock_ref[p] + total[:, p * width : (p + 1) * width]).astype(jnp.bfloat16)


def cycle_sum(at, fock_part, amps, ints):
    pairs, width, cols = fock_part.shape
    block = pl.BlockSpec((pairs, ROWS, cols), lambda r, at: (0, r, 0))
    whole = pl.BlockSpec(ints[0].shape, lambda r, at: (0, 0, 0, 0))
    return pl.pallas_call(
        cycle_kernel,
        out_shape=jax.ShapeDtypeStruct((pairs, width, cols), jnp.bfloat16),
        grid_spec=pltpu.PrefetchScalarGridSpec(
            num_scalar_prefetch=1,
            grid=(width // ROWS,),
            in_specs=[block] * (1 + 4 * NX) + [whole] * NY,
            out_specs=block,
            scratch_shapes=[pltpu.VMEM((NY,) + ints[0].shape, jnp.bfloat16)],
        ),
        compiler_params=pltpu.CompilerParams(vmem_limit_bytes=32 * MIB),
        cost_estimate=pl.CostEstimate(
            flops=2 * width * 4 * width * pairs * cols, bytes_accessed=12 * MIB, transcendentals=0
        ),
    )(at, fock_part, *amps, *ints)


def body(amplitudes, fock_vv, cycle_ints, tile_mask):
    amp, ints = lax.axis_index("amp"), lax.axis_index("ints")
    at = jnp.stack([amp // NZ, amp % NZ, ints // 2, ints % 2]).astype(jnp.int32)
    occ, depth, _, cols = cycle_ints.shape
    block = fock_vv.shape[0] // tile_mask.shape[0]

    present = lax.dynamic_slice(
        tile_mask, (amp * depth // block, ints * cols // block), (1, cols // block)
    )
    present = jnp.repeat(present[0].astype(jnp.bfloat16), block)
    masked = cycle_ints * present
    halves = masked.reshape(occ, depth, 2, 2 * cols).transpose(2, 0, 1, 3)
    to_z = jnp.broadcast_to(halves[None], (NZ // 2,) + halves.shape)
    to_z = to_z.reshape((NZ,) + halves.shape[1:])
    row = lax.all_to_all(to_z, "amp", 0, 0, tiled=True, axis_index_groups=Z_GROUPS)
    ints_by_y = [row] + [lax.ppermute(row, "amp", Y_RING(-e)) for e in (1, 2, 3)]

    own = [amplitudes] + [lax.ppermute(amplitudes, "ints", X_RING(-d)) for d in (1, 2, 3)]
    partner = lax.ppermute(amplitudes, "amp", Z_PAIR)
    other = [
        partner,
        lax.ppermute(partner, "ints", X_RING(-1)),
        lax.ppermute(own[2], "amp", Z_PAIR),
        lax.ppermute(partner, "ints", X_RING(-3)),
    ]
    own_swapped = [lax.ppermute(t, "ints", CORES) for t in own]
    other_swapped = [lax.ppermute(t, "ints", CORES) for t in other]

    fock_part = fock_terms(at, fock_vv, amplitudes, own, own_swapped)
    return cycle_sum(at, fock_part, own + own_swapped + other + other_swapped, ints_by_y)


def solution(mesh):
    in_specs = (P("amp", None, "ints"), P(), P(None, "amp", None, "ints"), P())
    out_specs = P("amp", None, "ints")
    return jax.shard_map(body, mesh=mesh, in_specs=in_specs, out_specs=out_specs, check_vma=False)
```

time: 190 us -> 92.2 us (0.49)
  the two profiles are of different devices: /device:TPU:8 before, /device:TPU:17 now
where the time goes in v1:
time: 92.2 us; the launch traced here: 91.9 us
  starting transfers between devices  42.3 us (46%)
  waiting for transfers between devices  31.7 us (34%)
  Pallas kernels  12.1 us (13%)
  local copies, waits for them, and re-layouts  3.84 us (4%)
  other arithmetic  1.8 us (2%)
    ppermute x4, starting transfers between devices, body(): other_swapped = [lax.ppermute(t, 'ints', CORES) for t in other]  19 us
    ppermute x1, waiting for transfers between devices, body(): partner = lax.ppermute(amplitudes, 'amp', Z_PAIR)  8.69 us
    all_to_all x1, starting transfers between devices, body(): lax.all_to_all(to_z, 'amp', 0, 0, tiled=True, axis_index_groups=Z_GROUPS)  8.19 us
    ppermute x3, waiting for transfers between devices, body(): lax.ppermute(amplitudes, 'ints', X_RING(-d))  8.13 us
    pallas_call x1, Pallas kernels, cycle_sum(): pl.pallas_call(cycle_kernel, out_shape=jax.ShapeDtypeStruct((pairs, width...  7.35 us
    ppermute x1, waiting for transfers between devices, body(): lax.ppermute(own[2], 'amp', Z_PAIR)  7.2 us
    ppermute x3, starting transfers between devices, body(): lax.ppermute(amplitudes, 'ints', X_RING(-d))  4.91 us
    pallas_call x1, Pallas kernels, fock_terms(): pl.pallas_call(fock_kernel, out_shape=jax.ShapeDtypeStruct((pairs, width,...  4.77 us
  transfers between devices with their start and end apart: 19, of which 5 were waited for; matrix products, arithmetic and copies ran while one was open for 3% of the time, Pallas kernels for 5%

profile of v1, /device:TPU:17, one launch (start us, length us, event | category | flops | bytes accessed | tf_op | source)
XLA Modules:
  0.0 91.9 jit_solution(2618845539633971041)
XLA Ops:
  0.0 0.7 collective-permute-start.3
  0.7 1.2 %collective-permute-start.2 = (bf16[2,1024,128]{2,1,0:T(8,128)(2,1)}, bf16[2,1024,128]{2,1,0:T(8,128)(2,1)}, u32[]{:S(2)}, u32[]{:S(2)}) collective-permute-start(bf16[2,1024,128]{2,1,0:T(8,128)(2,1)} %refs_0_.3), channel_id=1, source_target_pairs={{0,2},{1,3},{2,4},{3,5},{4,6},{5,7},{6,0},{7,1},{8,10},{9,11},{10,... | collective-permute-start | bytes 1572872 | tf_op jit(solution)/shard_map/ppermute | solution.py:134
  1.9 2.5 %collective-permute-start.1 = (bf16[2,1024,128]{2,1,0:T(8,128)(2,1)}, bf16[2,1024,128]{2,1,0:T(8,128)(2,1)}, u32[]{:S(2)}, u32[]{:S(2)}) collective-permute-start(bf16[2,1024,128]{2,1,0:T(8,128)(2,1)} %refs_0_.3), channel_id=1, source_target_pairs={{0,4},{1,5},{2,6},{3,7},{4,0},{5,1},{6,2},{7,3},{8,12},{9,13},{10,... | collective-permute-start | bytes 1572872 | tf_op jit(solution)/shard_map/ppermute | solution.py:134
  4.4 0.8 convert_bitcast_fusion
  5.3 1.0 %broadcast_multiply_fusion = bf16[4,32,4,128]{3,2,1,0:T(4,128)(2,1)S(1)} fusion(bf16[4,32,4,128]{3,2,1,0:T(4,128)(2,1)} %param.6, bf16[128]{0:T(256)(128)(2,1)S(1)} %mul.18), kind=kLoop, calls=%fused_computation | loop fusion | flops 65536 | bytes 262400 | tf_op jit(solution)/shard_map/mul | solution.py:127
  6.2 0.1 reshape.9
  6.4 0.9 broadcast_in_dim.10
  7.2 8.2 %all-to-all-start = ((bf16[8,4,32,256]{3,2,1,0:T(8,128)(2,1)}), bf16[8,4,32,256]{3,2,1,0:T(8,128)(2,1)}, u32[]{:S(2)}, u32[]{:S(2)}) async-start(bf16[8,4,32,256]{3,2,1,0:T(8,128)(2,1)} %bitcast.8), calls=%async_computation | async-start | bytes 1048576 | tf_op jit(solution)/shard_map/all_to_all | solution.py:131
  15.4 1.2 %collective-permute-start = (bf16[2,1024,128]{2,1,0:T(8,128)(2,1)S(1)}, bf16[2,1024,128]{2,1,0:T(8,128)(2,1)}, u32[]{:S(2)}, u32[]{:S(2)}) collective-permute-start(bf16[2,1024,128]{2,1,0:T(8,128)(2,1)S(1)} %copy-done.1), channel_id=1, source_target_pairs={{0,6},{1,7},{2,0},{3,1},{4,2},{5,3},{6,4},{7,5},{8,14},{9,15},{10,... | collective-permute-start | bytes 1572872 | tf_op jit(solution)/shard_map/ppermute | solution.py:134
  16.7 1.4 %collective-permute-start.7 = (bf16[2,1024,128]{2,1,0:T(8,128)(2,1)S(1)}, bf16[2,1024,128]{2,1,0:T(8,128)(2,1)}, u32[]{:S(2)}, u32[]{:S(2)}) collective-permute-start(bf16[2,1024,128]{2,1,0:T(8,128)(2,1)S(1)} %copy-done.1), channel_id=1, source_target_pairs={{0,8},{8,0},{16,24},{24,16},{32,40},{40,32},{48,56},{56,48},{64,72... | collective-permute-start | bytes 1572872 | tf_op jit(solution)/shard_map/ppermute | solution.py:135
  18.0 1.8 %collective-permute-start.6 = (bf16[2,1024,128]{2,1,0:T(8,128)(2,1)}, bf16[2,1024,128]{2,1,0:T(8,128)(2,1)S(1)}, u32[]{:S(2)}, u32[]{:S(2)}) collective-permute-start(bf16[2,1024,128]{2,1,0:T(8,128)(2,1)} %collective-permute-done.2.refs_3_), channel_id=1, source_target_pairs={{0,1},{1,0},{2,3},{3,2},{4,5},{5,4},{6,7},{7,6},{8,9},{9,8},{10,11... | collective-permute-start | bytes 1572872 | tf_op jit(solution)/shard_map/ppermute | solution.py:142
  19.8 8.1 %collective-permute-done.1.refs_2_ = bf16[2,1024,128]{2,1,0:T(8,128)(2,1)} collective-permute-done((bf16[2,1024,128]{2,1,0:T(8,128)(2,1)}, bf16[2,1024,128]{2,1,0:T(8,128)(2,1)}, u32[]{:S(2)}, u32[]{:S(2)}) %collective-permute-start.1) | collective-permute-done | bytes 524320 | tf_op jit(solution)/shard_map/ppermute | solution.py:134
  27.9 1.6 %collective-permute-start.9 = (bf16[2,1024,128]{2,1,0:T(8,128)(2,1)}, bf16[2,1024,128]{2,1,0:T(8,128)(2,1)}, u32[]{:S(2)}, u32[]{:S(2)}) collective-permute-start(bf16[2,1024,128]{2,1,0:T(8,128)(2,1)} %collective-permute-done.1.refs_2_), channel_id=1, source_target_pairs={{0,8},{8,0},{16,24},{24,16},{32,40},{40,32},{48,56},{56,48},{64,72... | collective-permute-start | bytes 1572872 | tf_op jit(solution)/shard_map/ppermute | solution.py:139
  29.6 1.1 %collective-permute-start.5 = (bf16[2,1024,128]{2,1,0:T(8,128)(2,1)}, bf16[2,1024,128]{2,1,0:T(8,128)(2,1)}, u32[]{:S(2)}, u32[]{:S(2)}) collective-permute-start(bf16[2,1024,128]{2,1,0:T(8,128)(2,1)} %collective-permute-done.1.refs_2_), channel_id=1, source_target_pairs={{0,1},{1,0},{2,3},{3,2},{4,5},{5,4},{6,7},{7,6},{8,9},{9,8},{10,11... | collective-permute-start | bytes 1572872 | tf_op jit(solution)/shard_map/ppermute | solution.py:142
  30.7 0.1 collective-permute-start.4
  30.8 8.7 %collective-permute-done.7.refs_8_ = bf16[2,1024,128]{2,1,0:T(8,128)(2,1)} collective-permute-done((bf16[2,1024,128]{2,1,0:T(8,128)(2,1)S(1)}, bf16[2,1024,128]{2,1,0:T(8,128)(2,1)}, u32[]{:S(2)}, u32[]{:S(2)}) %collective-permute-start.7) | collective-permute-done | bytes 524320 | tf_op jit(solution)/shard_map/ppermute | solution.py:135
  39.5 3.2 %collective-permute-start.11 = (bf16[2,1024,128]{2,1,0:T(8,128)(2,1)}, bf16[2,1024,128]{2,1,0:T(8,128)(2,1)}, u32[]{:S(2)}, u32[]{:S(2)}) collective-permute-start(bf16[2,1024,128]{2,1,0:T(8,128)(2,1)} %collective-permute-done.7.refs_8_), channel_id=1, source_target_pairs={{0,1},{1,0},{2,3},{3,2},{4,5},{5,4},{6,7},{7,6},{8,9},{9,8},{10,11... | collective-permute-start | bytes 1572872 | tf_op jit(solution)/shard_map/ppermute | solution.py:143
  42.7 0.8 copy-done.2
  43.5 7.2 %collective-permute-done.9.refs_10_ = bf16[2,1024,128]{2,1,0:T(8,128)(2,1)} collective-permute-done((bf16[2,1024,128]{2,1,0:T(8,128)(2,1)}, bf16[2,1024,128]{2,1,0:T(8,128)(2,1)}, u32[]{:S(2)}, u32[]{:S(2)}) %collective-permute-start.9) | collective-permute-done | bytes 524320 | tf_op jit(solution)/shard_map/ppermute | solution.py:139
  50.7 1.2 %collective-permute-start.8 = (bf16[2,1024,128]{2,1,0:T(8,128)(2,1)}, bf16[2,1024,128]{2,1,0:T(8,128)(2,1)}, u32[]{:S(2)}, u32[]{:S(2)}) collective-permute-start(bf16[2,1024,128]{2,1,0:T(8,128)(2,1)} %collective-permute-done.7.refs_8_), channel_id=1, source_target_pairs={{0,6},{1,7},{2,0},{3,1},{4,2},{5,3},{6,4},{7,5},{8,14},{9,15},{10,... | collective-permute-start | bytes 1572872 | tf_op jit(solution)/shard_map/ppermute | solution.py:138
  51.9 1.0 %collective-permute-start.17 = (bf16[8,4,32,256]{3,2,1,0:T(8,128)(2,1)}, bf16[8,4,32,256]{3,2,1,0:T(8,128)(2,1)S(1)}, u32[]{:S(2)}, u32[]{:S(2)}) collective-permute-start(bf16[8,4,32,256]{3,2,1,0:T(8,128)(2,1)} %all-to-all-done.refs_16_), channel_id=1, source_target_pairs={{0,64},{8,72},{16,80},{24,88},{32,96},{40,104},{48,112},{56,120},{... | collective-permute-start | bytes 1572872 | tf_op jit(solution)/shard_map/ppermute | solution.py:132
  52.9 0.3 collective-permute-start.16
  53.2 0.9 %collective-permute-start.15 = (bf16[8,4,32,256]{3,2,1,0:T(8,128)(2,1)}, bf16[8,4,32,256]{3,2,1,0:T(8,128)(2,1)}, u32[]{:S(2)}, u32[]{:S(2)}) collective-permute-start(bf16[8,4,32,256]{3,2,1,0:T(8,128)(2,1)} %all-to-all-done.refs_16_), channel_id=1, source_target_pairs={{0,192},{8,200},{16,208},{24,216},{32,224},{40,232},{48,240},{56,2... | collective-permute-start | bytes 1572872 | tf_op jit(solution)/shard_map/ppermute | solution.py:132
  54.2 4.4 %collective-permute-done.10.refs_11_ = bf16[2,1024,128]{2,1,0:T(8,128)(2,1)} collective-permute-done((bf16[2,1024,128]{2,1,0:T(8,128)(2,1)}, bf16[2,1024,128]{2,1,0:T(8,128)(2,1)}, u32[]{:S(2)}, u32[]{:S(2)}) %collective-permute-start.10) | collective-permute-done | bytes 524320 | tf_op jit(solution)/shard_map/ppermute | solution.py:140
  58.6 0.8 collective-permute-start.13
  59.4 3.3 %collective-permute-done.8.refs_9_ = bf16[2,1024,128]{2,1,0:T(8,128)(2,1)} collective-permute-done((bf16[2,1024,128]{2,1,0:T(8,128)(2,1)}, bf16[2,1024,128]{2,1,0:T(8,128)(2,1)}, u32[]{:S(2)}, u32[]{:S(2)}) %collective-permute-start.8) | collective-permute-done | bytes 524320 | tf_op jit(solution)/shard_map/ppermute | solution.py:138
  62.6 2.7 %collective-permute-start.14 = (bf16[2,1024,128]{2,1,0:T(8,128)(2,1)}, bf16[2,1024,128]{2,1,0:T(8,128)(2,1)}, u32[]{:S(2)}, u32[]{:S(2)}) collective-permute-start(bf16[2,1024,128]{2,1,0:T(8,128)(2,1)} %collective-permute-done.10.refs_11_), channel_id=1, source_target_pairs={{0,1},{1,0},{2,3},{3,2},{4,5},{5,4},{6,7},{7,6},{8,9},{9,8},{10,11... | collective-permute-start | bytes 1572872 | tf_op jit(solution)/shard_map/ppermute | solution.py:143
  65.4 0.9 copy-done.5
  66.2 12.3 %collective-permute-start.12 = (bf16[2,1024,128]{2,1,0:T(8,128)(2,1)}, bf16[2,1024,128]{2,1,0:T(8,128)(2,1)}, u32[]{:S(2)}, u32[]{:S(2)}) collective-permute-start(bf16[2,1024,128]{2,1,0:T(8,128)(2,1)} %collective-permute-done.8.refs_9_), channel_id=1, source_target_pairs={{0,1},{1,0},{2,3},{3,2},{4,5},{5,4},{6,7},{7,6},{8,9},{9,8},{10,11... | collective-permute-start | bytes 1572872 | tf_op jit(solution)/shard_map/ppermute | solution.py:143
  78.6 1.0 %copy-done.3 = bf16[2,1024,128]{2,1,0:T(8,128)(2,1)S(1)} copy-done((bf16[2,1024,128]{2,1,0:T(8,128)(2,1)S(1)}, bf16[2,1024,128]{2,1,0:T(8,128)(2,1)}, u32[]{:S(2)}) %copy-start.3) | copy-done | bytes 524312
  79.7 4.8 %shard_map.46.fock_ref = f32[2,1024,128]{2,1,0:T(8,128)S(1)} custom-call(s32[4]{0:T(128)S(1)} %pad_add_fusion.at_ref, bf16[1024,1024]{1,0:T(8,128)(2,1)S(1)} %copy-done, bf16[1024,1024]{1,0:T(8,128)(2,1)S(1)} %copy-done, bf16[2,1024,128]{2,1,0:T(8,128)(2,1)S(1)} %copy-done.1, bf16[2,1024,128]{2,1,0:T(8,128)(2,1)S(1)} %copy-done.1, ...), custom_call_target="tpu_custom_call" | custom-call | flops 1073741824 | bytes 9437184 | tf_op jit(solution)/shard_map/pallas_call | solution.py:41
  84.5 7.3 %shard_map.47 = bf16[2,1024,128]{2,1,0:T(8,128)(2,1)} custom-call(s32[4]{0:T(128)S(1)} %pad_add_fusion.at_ref, f32[2,1024,128]{2,1,0:T(8,128)S(1)} %shard_map.46.fock_ref, bf16[2,1024,128]{2,1,0:T(8,128)(2,1)S(1)} %copy-done.1, bf16[2,1024,128]{2,1,0:T(8,128)(2,1)} %collective-permute-done.refs_1_, bf16[2,1024,128]{2,1,0:T(8,128)(2,1)} %collective-permute-done.1.refs_2_, ...), custom_call_target="tpu_custom_call" | custom-call | flops 2147483648 | bytes 12582912 | tf_op jit(solution)/shard_map/pallas_call | solution.py:100
  (30 shorter events, 0.3 us)
Async XLA Ops:
  0.0 15.4 %copy-start.1 = (bf16[2,1024,128]{2,1,0:T(8,128)(2,1)S(1)}, bf16[2,1024,128]{2,1,0:T(8,128)(2,1)}, u32[]{:S(2)}) copy-start(bf16[2,1024,128]{2,1,0:T(8,128)(2,1)} %refs_0_.3) | copy-start | bytes 1572868
  0.0 78.6 %copy-start = (bf16[1024,1024]{1,0:T(8,128)(2,1)S(1)}, bf16[1024,1024]{1,0:T(8,128)(2,1)}, u32[]{:S(2)}) copy-start(bf16[1024,1024]{1,0:T(8,128)(2,1)} %rows_ref.1) | copy-start | bytes 6291460
  0.0 29.6 %collective-permute-start.3 = (bf16[2,1024,128]{2,1,0:T(8,128)(2,1)}, bf16[2,1024,128]{2,1,0:T(8,128)(2,1)S(1)}, u32[]{:S(2)}, u32[]{:S(2)}) collective-permute-start(bf16[2,1024,128]{2,1,0:T(8,128)(2,1)} %refs_0_.3), channel_id=1, source_target_pairs={{0,1},{1,0},{2,3},{3,2},{4,5},{5,4},{6,7},{7,6},{8,9},{9,8},{10,11... | collective-permute-start | bytes 1572872 | tf_op jit(solution)/shard_map/ppermute | solution.py:142
  0.7 17.4 %collective-permute-start.2 = (bf16[2,1024,128]{2,1,0:T(8,128)(2,1)}, bf16[2,1024,128]{2,1,0:T(8,128)(2,1)}, u32[]{:S(2)}, u32[]{:S(2)}) collective-permute-start(bf16[2,1024,128]{2,1,0:T(8,128)(2,1)} %refs_0_.3), channel_id=1, source_target_pairs={{0,2},{1,3},{2,4},{3,5},{4,6},{5,7},{6,0},{7,1},{8,10},{9,11},{10,... | collective-permute-start | bytes 1572872 | tf_op jit(solution)/shard_map/ppermute | solution.py:134
  1.9 26.0 %collective-permute-start.1 = (bf16[2,1024,128]{2,1,0:T(8,128)(2,1)}, bf16[2,1024,128]{2,1,0:T(8,128)(2,1)}, u32[]{:S(2)}, u32[]{:S(2)}) collective-permute-start(bf16[2,1024,128]{2,1,0:T(8,128)(2,1)} %refs_0_.3), channel_id=1, source_target_pairs={{0,4},{1,5},{2,6},{3,7},{4,0},{5,1},{6,2},{7,3},{8,12},{9,13},{10,... | collective-permute-start | bytes 1572872 | tf_op jit(solution)/shard_map/ppermute | solution.py:134
  7.2 44.6 %all-to-all-start = ((bf16[8,4,32,256]{3,2,1,0:T(8,128)(2,1)}), bf16[8,4,32,256]{3,2,1,0:T(8,128)(2,1)}, u32[]{:S(2)}, u32[]{:S(2)}) async-start(bf16[8,4,32,256]{3,2,1,0:T(8,128)(2,1)} %bitcast.8), calls=%async_computation | async-start | bytes 1048576 | tf_op jit(solution)/shard_map/all_to_all | solution.py:131
  15.4 15.3 %collective-permute-start = (bf16[2,1024,128]{2,1,0:T(8,128)(2,1)S(1)}, bf16[2,1024,128]{2,1,0:T(8,128)(2,1)}, u32[]{:S(2)}, u32[]{:S(2)}) collective-permute-start(bf16[2,1024,128]{2,1,0:T(8,128)(2,1)S(1)} %copy-done.1), channel_id=1, source_target_pairs={{0,6},{1,7},{2,0},{3,1},{4,2},{5,3},{6,4},{7,5},{8,14},{9,15},{10,... | collective-permute-start | bytes 1572872 | tf_op jit(solution)/shard_map/ppermute | solution.py:134
  16.7 22.8 %collective-permute-start.7 = (bf16[2,1024,128]{2,1,0:T(8,128)(2,1)S(1)}, bf16[2,1024,128]{2,1,0:T(8,128)(2,1)}, u32[]{:S(2)}, u32[]{:S(2)}) collective-permute-start(bf16[2,1024,128]{2,1,0:T(8,128)(2,1)S(1)} %copy-done.1), channel_id=1, source_target_pairs={{0,8},{8,0},{16,24},{24,16},{32,40},{40,32},{48,56},{56,48},{64,72... | collective-permute-start | bytes 1572872 | tf_op jit(solution)/shard_map/ppermute | solution.py:135
  18.0 24.7 %collective-permute-start.6 = (bf16[2,1024,128]{2,1,0:T(8,128)(2,1)}, bf16[2,1024,128]{2,1,0:T(8,128)(2,1)S(1)}, u32[]{:S(2)}, u32[]{:S(2)}) collective-permute-start(bf16[2,1024,128]{2,1,0:T(8,128)(2,1)} %collective-permute-done.2.refs_3_), channel_id=1, source_target_pairs={{0,1},{1,0},{2,3},{3,2},{4,5},{5,4},{6,7},{7,6},{8,9},{9,8},{10,11... | collective-permute-start | bytes 1572872 | tf_op jit(solution)/shard_map/ppermute | solution.py:142
  27.9 22.8 %collective-permute-start.9 = (bf16[2,1024,128]{2,1,0:T(8,128)(2,1)}, bf16[2,1024,128]{2,1,0:T(8,128)(2,1)}, u32[]{:S(2)}, u32[]{:S(2)}) collective-permute-start(bf16[2,1024,128]{2,1,0:T(8,128)(2,1)} %collective-permute-done.1.refs_2_), channel_id=1, source_target_pairs={{0,8},{8,0},{16,24},{24,16},{32,40},{40,32},{48,56},{56,48},{64,72... | collective-permute-start | bytes 1572872 | tf_op jit(solution)/shard_map/ppermute | solution.py:139
  29.6 22.3 %collective-permute-start.5 = (bf16[2,1024,128]{2,1,0:T(8,128)(2,1)}, bf16[2,1024,128]{2,1,0:T(8,128)(2,1)}, u32[]{:S(2)}, u32[]{:S(2)}) collective-permute-start(bf16[2,1024,128]{2,1,0:T(8,128)(2,1)} %collective-permute-done.1.refs_2_), channel_id=1, source_target_pairs={{0,1},{1,0},{2,3},{3,2},{4,5},{5,4},{6,7},{7,6},{8,9},{9,8},{10,11... | collective-permute-start | bytes 1572872 | tf_op jit(solution)/shard_map/ppermute | solution.py:142
  30.7 22.2 %collective-permute-start.4 = (bf16[2,1024,128]{2,1,0:T(8,128)(2,1)}, bf16[2,1024,128]{2,1,0:T(8,128)(2,1)}, u32[]{:S(2)}, u32[]{:S(2)}) collective-permute-start(bf16[2,1024,128]{2,1,0:T(8,128)(2,1)} %collective-permute-done.refs_1_), channel_id=1, source_target_pairs={{0,1},{1,0},{2,3},{3,2},{4,5},{5,4},{6,7},{7,6},{8,9},{9,8},{10,11... | collective-permute-start | bytes 1572872 | tf_op jit(solution)/shard_map/ppermute | solution.py:142
  39.5 13.8 %collective-permute-start.11 = (bf16[2,1024,128]{2,1,0:T(8,128)(2,1)}, bf16[2,1024,128]{2,1,0:T(8,128)(2,1)}, u32[]{:S(2)}, u32[]{:S(2)}) collective-permute-start(bf16[2,1024,128]{2,1,0:T(8,128)(2,1)} %collective-permute-done.7.refs_8_), channel_id=1, source_target_pairs={{0,1},{1,0},{2,3},{3,2},{4,5},{5,4},{6,7},{7,6},{8,9},{9,8},{10,11... | collective-permute-start | bytes 1572872 | tf_op jit(solution)/shard_map/ppermute | solution.py:143
  42.7 0.8 copy-start.2
  43.5 15.1 %collective-permute-start.10 = (bf16[2,1024,128]{2,1,0:T(8,128)(2,1)}, bf16[2,1024,128]{2,1,0:T(8,128)(2,1)}, u32[]{:S(2)}, u32[]{:S(2)}) collective-permute-start(bf16[2,1024,128]{2,1,0:T(8,128)(2,1)} %collective-permute-done.7.refs_8_), channel_id=1, source_target_pairs={{0,2},{1,3},{2,4},{3,5},{4,6},{5,7},{6,0},{7,1},{8,10},{9,11},{10,... | collective-permute-start | bytes 1572872 | tf_op jit(solution)/shard_map/ppermute | solution.py:140
  50.7 11.9 %collective-permute-start.8 = (bf16[2,1024,128]{2,1,0:T(8,128)(2,1)}, bf16[2,1024,128]{2,1,0:T(8,128)(2,1)}, u32[]{:S(2)}, u32[]{:S(2)}) collective-permute-start(bf16[2,1024,128]{2,1,0:T(8,128)(2,1)} %collective-permute-done.7.refs_8_), channel_id=1, source_target_pairs={{0,6},{1,7},{2,0},{3,1},{4,2},{5,3},{6,4},{7,5},{8,14},{9,15},{10,... | collective-permute-start | bytes 1572872 | tf_op jit(solution)/shard_map/ppermute | solution.py:138
  51.9 13.5 %collective-permute-start.17 = (bf16[8,4,32,256]{3,2,1,0:T(8,128)(2,1)}, bf16[8,4,32,256]{3,2,1,0:T(8,128)(2,1)S(1)}, u32[]{:S(2)}, u32[]{:S(2)}) collective-permute-start(bf16[8,4,32,256]{3,2,1,0:T(8,128)(2,1)} %all-to-all-done.refs_16_), channel_id=1, source_target_pairs={{0,64},{8,72},{16,80},{24,88},{32,96},{40,104},{48,112},{56,120},{... | collective-permute-start | bytes 1572872 | tf_op jit(solution)/shard_map/ppermute | solution.py:132
  52.9 31.5 %collective-permute-start.16 = (bf16[8,4,32,256]{3,2,1,0:T(8,128)(2,1)}, bf16[8,4,32,256]{3,2,1,0:T(8,128)(2,1)}, u32[]{:S(2)}, u32[]{:S(2)}) collective-permute-start(bf16[8,4,32,256]{3,2,1,0:T(8,128)(2,1)} %all-to-all-done.refs_16_), channel_id=1, source_target_pairs={{0,128},{8,136},{16,144},{24,152},{32,160},{40,168},{48,176},{56,1... | collective-permute-start | bytes 1572872 | tf_op jit(solution)/shard_map/ppermute | solution.py:132
  53.2 31.2 %collective-permute-start.15 = (bf16[8,4,32,256]{3,2,1,0:T(8,128)(2,1)}, bf16[8,4,32,256]{3,2,1,0:T(8,128)(2,1)}, u32[]{:S(2)}, u32[]{:S(2)}) collective-permute-start(bf16[8,4,32,256]{3,2,1,0:T(8,128)(2,1)} %all-to-all-done.refs_16_), channel_id=1, source_target_pairs={{0,192},{8,200},{16,208},{24,216},{32,224},{40,232},{48,240},{56,2... | collective-permute-start | bytes 1572872 | tf_op jit(solution)/shard_map/ppermute | solution.py:132
  58.6 25.9 %collective-permute-start.13 = (bf16[2,1024,128]{2,1,0:T(8,128)(2,1)}, bf16[2,1024,128]{2,1,0:T(8,128)(2,1)}, u32[]{:S(2)}, u32[]{:S(2)}) collective-permute-start(bf16[2,1024,128]{2,1,0:T(8,128)(2,1)} %collective-permute-done.9.refs_10_), channel_id=1, source_target_pairs={{0,1},{1,0},{2,3},{3,2},{4,5},{5,4},{6,7},{7,6},{8,9},{9,8},{10,11... | collective-permute-start | bytes 1572872 | tf_op jit(solution)/shard_map/ppermute | solution.py:143
  62.6 21.8 %collective-permute-start.14 = (bf16[2,1024,128]{2,1,0:T(8,128)(2,1)}, bf16[2,1024,128]{2,1,0:T(8,128)(2,1)}, u32[]{:S(2)}, u32[]{:S(2)}) collective-permute-start(bf16[2,1024,128]{2,1,0:T(8,128)(2,1)} %collective-permute-done.10.refs_11_), channel_id=1, source_target_pairs={{0,1},{1,0},{2,3},{3,2},{4,5},{5,4},{6,7},{7,6},{8,9},{9,8},{10,11... | collective-permute-start | bytes 1572872 | tf_op jit(solution)/shard_map/ppermute | solution.py:143
  65.4 0.9 copy-start.5
  66.2 18.2 %collective-permute-start.12 = (bf16[2,1024,128]{2,1,0:T(8,128)(2,1)}, bf16[2,1024,128]{2,1,0:T(8,128)(2,1)}, u32[]{:S(2)}, u32[]{:S(2)}) collective-permute-start(bf16[2,1024,128]{2,1,0:T(8,128)(2,1)} %collective-permute-done.8.refs_9_), channel_id=1, source_target_pairs={{0,1},{1,0},{2,3},{3,2},{4,5},{5,4},{6,7},{7,6},{8,9},{9,8},{10,11... | collective-permute-start | bytes 1572872 | tf_op jit(solution)/shard_map/ppermute | solution.py:143
  78.6 1.0 %copy-start.3 = (bf16[2,1024,128]{2,1,0:T(8,128)(2,1)S(1)}, bf16[2,1024,128]{2,1,0:T(8,128)(2,1)}, u32[]{:S(2)}) copy-start(bf16[2,1024,128]{2,1,0:T(8,128)(2,1)} %copy-done.2) | copy-start | bytes 1572868
  79.6 4.8 %copy-start.4 = (bf16[2,1024,128]{2,1,0:T(8,128)(2,1)S(1)}, bf16[2,1024,128]{2,1,0:T(8,128)(2,1)}, u32[]{:S(2)}) copy-start(bf16[2,1024,128]{2,1,0:T(8,128)(2,1)} %copy-done.2) | copy-start | bytes 1572868
  79.6 4.8 %copy-start.6 = (bf16[8,4,32,256]{3,2,1,0:T(8,128)(2,1)S(1)}, bf16[8,4,32,256]{3,2,1,0:T(8,128)(2,1)}, u32[]{:S(2)}) copy-start(bf16[8,4,32,256]{3,2,1,0:T(8,128)(2,1)} %copy-done.5) | copy-start | bytes 1572868

commit v2 on v0

v2 whole, which is shorter than its diff:
```python
import functools

import jax
import jax.numpy as jnp
from jax import lax
from jax.experimental import pallas as pl
from jax.experimental.pallas import tpu as pltpu
from jax.sharding import PartitionSpec as P

NX, NY, NZ = 4, 4, 8
X_RING = lambda d: [(2 * x + c, 2 * ((x + d) % NX) + c) for x in range(NX) for c in range(2)]
Y_RING = lambda d: [(y * NZ + z, ((y + d) % NY) * NZ + z) for y in range(NY) for z in range(NZ)]
Z_PAIR = [(p, p ^ 1) for p in range(NY * NZ)]
CORES = [(q, q ^ 1) for q in range(2 * NX)]
X_GROUPS = [[2 * x + c for x in range(NX)] for c in range(2)]
Y_GROUPS = [[y * NZ + z for y in range(NY)] for z in range(NZ)]
Z_GROUPS = [[y * NZ + z for z in range(NZ)] for y in range(NY)]
ROWS = 256
MIB = 1 << 20


VM = 16
COST = 1


VMEM = pl.BlockSpec(memory_space=pltpu.VMEM)
SMEM = pl.BlockSpec(memory_space=pltpu.SMEM)


def fock_kernel(at_ref, fock_ref, rows_ref, *refs):
    amps, out_ref = refs[:-1], refs[-1]
    x, core = at_ref[2], at_ref[3]
    own = amps[0]
    width = own.shape[2]
    both = jnp.concatenate([own[0], own[1]], axis=1)
    fock = []
    for i in range(len(amps)):
        chip, c = lax.rem(x + i // 2, NX), (1 - core if i % 2 else core)
        start = pl.multiple_of((2 * chip + c) * width, width)
        fock.append(rows_ref[:, pl.ds(start, width)])
    fock = jnp.concatenate(fock, axis=1)

    @pl.loop(0, fock_ref.shape[0] // ROWS)
    def _(r):
        at = pl.ds(pl.multiple_of(r * ROWS, ROWS), ROWS)
        left = jnp.dot(fock_ref[at, :], both, preferred_element_type=jnp.float32)
        for p in range(2):
            rows = jnp.concatenate([a[p, at, :] for a in amps], axis=1)
            right = lax.dot_general(
                rows, fock, (((1,), (1,)), ((), ())), preferred_element_type=jnp.float32
            )
            out_ref[p, at, :] = left[:, p * width : (p + 1) * width] + right


def fock_terms(at, fock_vv, fock_rows, amps):
    pairs, width, cols = amps[0].shape
    return pl.pallas_call(
        fock_kernel,
        out_shape=jax.ShapeDtypeStruct((pairs, width, cols), jnp.float32),
        in_specs=[SMEM] + [VMEM] * (2 + len(amps)),
        out_specs=VMEM,
        compiler_params=pltpu.CompilerParams(vmem_limit_bytes=VM * MIB),
        cost_estimate=pl.CostEstimate(
            flops=2 * pairs * width * width * cols * 2, bytes_accessed=4 * MIB, transcendentals=0
        ),
    )(at, fock_vv, fock_rows, *amps)


def cycle_kernel(last, at_ref, *refs):
    fock_ref = sent_ref = None
    if last:
        fock_ref, sent_ref, refs = refs[0], refs[1], refs[2:]
    held, out_ref, refs = refs[-1], refs[-2], refs[:-2]
    ints, amps = refs[-NY:], refs[:-NY]
    y, x, core = at_ref[0], at_ref[2], at_ref[3]
    n_z, pairs, depth, cols = ints[0].shape
    side, width = n_z // 2, cols // 2
    for e in range(NY):
        d = lax.rem(y + e - x + 2 * NX, NX)
        for s in range(2):
            c = 1 - core if s else core
            for p in range(pairs):
                part = ints[e][pl.ds(c * side, side), p]
                held[d, s, p] = part.reshape(side * depth, cols)
    rhs = jnp.concatenate(
        [held[i // 2, i % 2, p] for p in range(pairs) for i in range(len(amps))], axis=0
    )

    @pl.loop(0, out_ref.shape[1] // ROWS)
    def _(r):
        at = pl.ds(pl.multiple_of(r * ROWS, ROWS), ROWS)
        lhs = jnp.concatenate([a[p, at, :] for p in range(pairs) for a in amps], axis=1)
        total = jnp.dot(lhs, rhs, preferred_element_type=jnp.float32)
        for p in range(pairs):
            mine_p = total[:, p * width : (p + 1) * width]
            if last:
                mine_p = mine_p + sent_ref[p, at, :].astype(jnp.float32)
                mine_p = mine_p.astype(jnp.bfloat16).astype(jnp.float32) + fock_ref[p, at, :]
            out_ref[p, at, :] = mine_p.astype(out_ref.dtype)


def cycle_sum(at, before, amps, ints, shape, cost):
    n_z, pairs, depth, cols = ints[0].shape
    last = bool(before)
    return pl.pallas_call(
        functools.partial(cycle_kernel, last),
        out_shape=jax.ShapeDtypeStruct(shape, jnp.bfloat16),
        in_specs=[SMEM] + [VMEM] * (len(before) + len(amps) + len(ints)),
        out_specs=VMEM,
        scratch_shapes=[pltpu.VMEM((NY, 2, pairs, n_z // 2 * depth, cols), jnp.bfloat16)],
        compiler_params=pltpu.CompilerParams(vmem_limit_bytes=VM * MIB),
        cost_estimate=pl.CostEstimate(
            flops=cost * shape[0] * shape[1] * shape[1] * shape[2] * 4,
            bytes_accessed=6 * MIB,
            transcendentals=0,
        ),
    )(at, *before, *amps, *ints)


def prepare_kernel(at_ref, mask_ref, ints_ref, out_ref):
    occ, depth, n_j, cols = ints_ref.shape
    block = n_j * NZ * NY * depth // n_j // mask_ref.shape[0]
    amp, q = at_ref[0] * NZ + at_ref[1], 2 * at_ref[2] + at_ref[3]
    place = lax.broadcasted_iota(jnp.int32, (depth, cols), 1) // block
    keep = jnp.zeros((depth, cols), jnp.float32)
    for b in range(cols // block):
        present = mask_ref[amp * depth // block, q * (cols // block) + b].astype(jnp.float32)
        keep = jnp.where(place == b, present, keep)
    keep = keep.astype(jnp.bfloat16)
    for k in range(occ):
        for j in range(2):
            pair = [ints_ref[k, :, 2 * j + p, :] * keep for p in range(2)]
            pair = jnp.concatenate(pair, axis=1)
            part = int(j == k // 2)
            for z in range(k // 2, NZ, 2):
                out_ref[part, z, k % 2] = pair


def prepare(at, tile_mask, cycle_ints):
    occ, depth, _, cols = cycle_ints.shape
    shape = (2, NZ, occ // 2, depth, 2 * cols)
    return pl.pallas_call(
        prepare_kernel,
        out_shape=jax.ShapeDtypeStruct(shape, jnp.bfloat16),
        grid_spec=pltpu.PrefetchScalarGridSpec(
            num_scalar_prefetch=2,
            grid=(1,),
            in_specs=[pl.BlockSpec(cycle_ints.shape, lambda r, at, mask: (0, 0, 0, 0))],
            out_specs=pl.BlockSpec(shape, lambda r, at, mask: (0, 0, 0, 0, 0)),
        ),
        compiler_params=pltpu.CompilerParams(vmem_limit_bytes=16 * MIB),
    )(at, tile_mask, cycle_ints)


def swap(a):
    return lax.ppermute(a, "ints", CORES)


def along_z(a):
    return lax.all_to_all(a, "amp", 0, 0, tiled=True, axis_index_groups=Z_GROUPS)


def along_y(row):
    return [row] + [lax.ppermute(row, "amp", Y_RING(-e)) for e in (1, 2, 3)]


def body(amplitudes, fock_vv, cycle_ints, tile_mask):
    amp, ints = lax.axis_index("amp"), lax.axis_index("ints")
    at = jnp.stack([amp // NZ, amp % NZ, ints // 2, ints % 2]).astype(jnp.int32)
    to_z = prepare(at, tile_mask, cycle_ints)
    rows = [along_z(to_z[0]), along_z(to_z[1])]
    partners, mine = along_y(rows[0]), along_y(rows[1])
    own = [amplitudes] + [lax.ppermute(amplitudes, "ints", X_RING(-d)) for d in (1, 2, 3)]
    own = [b for a in own for b in (a, swap(a))]

    fock_rows = lax.dynamic_slice_in_dim(fock_vv, ints * amplitudes.shape[2], amplitudes.shape[2], 0)
    fock_part = fock_terms(at, fock_vv, fock_rows, own)
    sent = cycle_sum(at, [], own, partners, amplitudes.shape, COST)
    sent = lax.ppermute(sent, "amp", Z_PAIR)
    return cycle_sum(at, [fock_part, sent], own, mine, amplitudes.shape, 1)


def solution(mesh):
    in_specs = (P("amp", None, "ints"), P(), P(None, "amp", None, "ints"), P())
    out_specs = P("amp", None, "ints")
    return jax.shard_map(body, mesh=mesh, in_specs=in_specs, out_specs=out_specs, check_vma=False)
```

time: 190 us -> 71.8 us (0.38)
  waiting for transfers between devices: 106 us -> 22.1 us
  blocking collectives: 28.6 us -> 0 us
  starting transfers between devices: 10.3 us -> 29.6 us
  between operations: 13.2 us -> 0.09 us
  matrix products: 13 us -> 0 us
  Pallas kernels: 0 us -> 12.8 us
  other arithmetic: 7.25 us -> 0.08 us
  local copies, waits for them, and re-layouts: 9.03 us -> 6.64 us
    all_gather x3 -> x0, waiting for transfers between devices: 90.8 us -> none  [the longest x1 54.2 us: body(): ints_full = lax.all_gather(cycle_ints, 'amp', axis=1, tiled=True)]
    all_to_all x1 -> x0, blocking collectives: 28.6 us -> none  [body(): lax.all_to_all(amplitudes, 'amp', split_axis=1, concat_axis=0, tiled=True)]
    ppermute x0 -> x14, starting transfers between devices: none -> 17.1 us  [the longest x6 10.2 us: along_y(): return [row] + [lax.ppermute(row, 'amp', Y_RING(-e)) for e in (1, 2, 3)]]
    dot_general x4 -> x0, matrix products: 13 us -> none  [the longest x1 5.84 us: body(): jnp.einsum('ikac,kcjb->ijab', grouped, masked, preferred_element_type=jnp...]
    pallas_call x0 -> x4, Pallas kernels: none -> 12.8 us  [the longest x2 8.25 us: cycle_sum(): pl.pallas_call(functools.partial(cycle_kernel, last), out_shape=jax.Shape...]
    ppermute x0 -> x14, waiting for transfers between devices: none -> 10.4 us  [the longest x6 10.4 us: along_y(): return [row] + [lax.ppermute(row, 'amp', Y_RING(-e)) for e in (1, 2, 3)]]
    convert_element_type x4 -> x0, local copies, waits for them, and re-layouts: 6.52 us -> none  [the longest x2 3.63 us: body(): total = left_term + right_term + returned.astype(jnp.float32)]
    mul x1 -> x0, other arithmetic: 6.07 us -> none  [body(): masked = ints_full * expanded.astype(jnp.bfloat16)[None, :, None, :]]
  transfers between devices with their start and end apart: 4 -> 16, of which waited for: 4 -> 6; matrix products, arithmetic and copies ran while one was open for 12% -> 3% of each run, Pallas kernels for 0% -> 12%
where the time goes in v2:
time: 71.8 us; the launch traced here: 71.3 us
  starting transfers between devices  29.6 us (41%)
  waiting for transfers between devices  22.1 us (31%)
  Pallas kernels  12.8 us (18%)
  local copies, waits for them, and re-layouts  6.64 us (9%)
    all_to_all x2, starting transfers between devices, along_z(): lax.all_to_all(a, 'amp', 0, 0, tiled=True, axis_index_groups=Z_GROUPS)  12.5 us
    all_to_all x2, waiting for transfers between devices, along_z(): lax.all_to_all(a, 'amp', 0, 0, tiled=True, axis_index_groups=Z_GROUPS)  11.6 us
    ppermute x6, waiting for transfers between devices, along_y(): return [row] + [lax.ppermute(row, 'amp', Y_RING(-e)) for e in (1, 2, 3)]  10.4 us
    ppermute x6, starting transfers between devices, along_y(): return [row] + [lax.ppermute(row, 'amp', Y_RING(-e)) for e in (1, 2, 3)]  10.2 us
    pallas_call x2, Pallas kernels, cycle_sum(): pl.pallas_call(functools.partial(cycle_kernel, last), out_shape=jax.Shape...  8.25 us
    ppermute x3, starting transfers between devices, body(): lax.ppermute(amplitudes, 'ints', X_RING(-d))  5.65 us
    unnamed x12, local copies, waits for them, and re-layouts  4.84 us
    pallas_call x1, Pallas kernels, fock_terms(): pl.pallas_call(fock_kernel, out_shape=jax.ShapeDtypeStruct((pairs, width,...  3.61 us
  transfers between devices with their start and end apart: 16, of which 6 were waited for; matrix products, arithmetic and copies ran while one was open for 3% of the time, Pallas kernels for 12%

profile of v2, /device:TPU:8, one launch (start us, length us, event | category | flops | bytes accessed | tf_op | source)
XLA Modules:
  0.0 71.3 jit_solution(7127862836440799017)
XLA Ops:
  0.0 1.5 %collective-permute-start.5 = (bf16[2,1024,128]{2,1,0:T(8,128)(2,1)}, bf16[2,1024,128]{2,1,0:T(8,128)(2,1)S(1)}, u32[]{:S(2)}, u32[]{:S(2)}) collective-permute-start(bf16[2,1024,128]{2,1,0:T(8,128)(2,1)} %refs_2_.1), channel_id=1, source_target_pairs={{0,2},{1,3},{2,4},{3,5},{4,6},{5,7},{6,0},{7,1},{8,10},{9,11},{10,... | collective-permute-start | bytes 1572872 | tf_op jit(solution)/shard_map/ppermute | solution.py:173
  1.5 2.7 %collective-permute-start.3 = (bf16[2,1024,128]{2,1,0:T(8,128)(2,1)}, bf16[2,1024,128]{2,1,0:T(8,128)(2,1)S(1)}, u32[]{:S(2)}, u32[]{:S(2)}) collective-permute-start(bf16[2,1024,128]{2,1,0:T(8,128)(2,1)} %refs_2_.1), channel_id=1, source_target_pairs={{0,4},{1,5},{2,6},{3,7},{4,0},{5,1},{6,2},{7,3},{8,12},{9,13},{10,... | collective-permute-start | bytes 1572872 | tf_op jit(solution)/shard_map/ppermute | solution.py:173
  4.2 1.4 %collective-permute-start.1 = (bf16[2,1024,128]{2,1,0:T(8,128)(2,1)}, bf16[2,1024,128]{2,1,0:T(8,128)(2,1)S(1)}, u32[]{:S(2)}, u32[]{:S(2)}) collective-permute-start(bf16[2,1024,128]{2,1,0:T(8,128)(2,1)} %refs_2_.1), channel_id=1, source_target_pairs={{0,6},{1,7},{2,0},{3,1},{4,2},{5,3},{6,4},{7,5},{8,14},{9,15},{10,... | collective-permute-start | bytes 1572872 | tf_op jit(solution)/shard_map/ppermute | solution.py:173
  5.7 0.1 pad_add_fusion.at_ref
  5.7 0.9 %copy-done.4 = bf16[4,32,4,128]{3,2,1,0:T(4,128)(2,1)S(1)} copy-done((bf16[4,32,4,128]{3,2,1,0:T(4,128)(2,1)S(1)}, bf16[4,32,4,128]{3,2,1,0:T(4,128)(2,1)}, u32[]{:S(2)}) %copy-start.4) | copy-done | bytes 131096
  6.6 0.7 copy-done.5
  7.3 0.9 %shard_map.47 = bf16[2,8,2,32,256]{4,3,2,1,0:T(8,128)(2,1)S(1)} custom-call(s32[4]{0:T(128)S(1)} %pad_add_fusion.at_ref, s32[16,16]{1,0:T(8,128)S(1)} %copy-done.5, bf16[4,32,4,128]{3,2,1,0:T(4,128)(2,1)S(1)} %copy-done.4), custom_call_target="tpu_custom_call" | custom-call | tf_op jit(solution)/shard_map/pallas_call | solution.py:142
  8.2 0.8 %slice_bitcast_fusion = (bf16[8,2,32,256]{3,2,1,0:T(8,128)(2,1)}, bf16[8,2,32,256]{3,2,1,0:T(8,128)(2,1)}) fusion(bf16[2,8,2,32,256]{4,3,2,1,0:T(8,128)(2,1)S(1)} %shard_map.47), kind=kLoop, calls=%fused_computation | loop fusion | bytes 1048576 | tf_op jit(solution)/shard_map/squeeze | solution.py:171
  9.1 8.5 %all-to-all-start = ((bf16[8,2,32,256]{3,2,1,0:T(8,128)(2,1)}), bf16[8,2,32,256]{3,2,1,0:T(8,128)(2,1)S(1)}, u32[]{:S(2)}, u32[]{:S(2)}) async-start(bf16[8,2,32,256]{3,2,1,0:T(8,128)(2,1)} %get-tuple-element.6), calls=%async_computation | async-start | bytes 524288 | tf_op jit(solution)/shard_map/all_to_all | solution.py:160
  17.5 0.1 collective-permute-start
  17.6 10.9 %all-to-all-done.refs_8_ = bf16[8,2,32,256]{3,2,1,0:T(8,128)(2,1)S(1)} async-done(((bf16[8,2,32,256]{3,2,1,0:T(8,128)(2,1)}), bf16[8,2,32,256]{3,2,1,0:T(8,128)(2,1)S(1)}, u32[]{:S(2)}, u32[]{:S(2)}) %all-to-all-start) | async-done | bytes 262176 | tf_op jit(solution)/shard_map/all_to_all | solution.py:160
  28.6 1.6 %collective-permute-start.9 = (bf16[8,2,32,256]{3,2,1,0:T(8,128)(2,1)S(1)}, bf16[8,2,32,256]{3,2,1,0:T(8,128)(2,1)S(1)}, u32[]{:S(2)}, u32[]{:S(2)}) collective-permute-start(bf16[8,2,32,256]{3,2,1,0:T(8,128)(2,1)S(1)} %all-to-all-done.refs_8_), channel_id=1, source_target_pairs={{0,64},{8,72},{16,80},{24,88},{32,96},{40,104},{48,112},{56,120},{... | collective-permute-start | bytes 786440 | tf_op jit(solution)/shard_map/ppermute | solution.py:164
  30.2 0.5 collective-permute-start.4
  30.7 0.1 collective-permute-start.2
  30.8 0.9 %collective-permute-start.8 = (bf16[8,2,32,256]{3,2,1,0:T(8,128)(2,1)S(1)}, bf16[8,2,32,256]{3,2,1,0:T(8,128)(2,1)}, u32[]{:S(2)}, u32[]{:S(2)}) collective-permute-start(bf16[8,2,32,256]{3,2,1,0:T(8,128)(2,1)S(1)} %all-to-all-done.refs_8_), channel_id=1, source_target_pairs={{0,128},{8,136},{16,144},{24,152},{32,160},{40,168},{48,176},{56,1... | collective-permute-start | bytes 786440 | tf_op jit(solution)/shard_map/ppermute | solution.py:164
  31.7 3.2 %collective-permute-done.9.refs_11_ = bf16[8,2,32,256]{3,2,1,0:T(8,128)(2,1)S(1)} collective-permute-done((bf16[8,2,32,256]{3,2,1,0:T(8,128)(2,1)S(1)}, bf16[8,2,32,256]{3,2,1,0:T(8,128)(2,1)S(1)}, u32[]{:S(2)}, u32[]{:S(2)}) %collective-permute-start.9) | collective-permute-done | bytes 262176 | tf_op jit(solution)/shard_map/ppermute | solution.py:164
  34.9 0.7 copy-done.2
  35.6 2.6 %collective-permute-start.7 = (bf16[8,2,32,256]{3,2,1,0:T(8,128)(2,1)S(1)}, bf16[8,2,32,256]{3,2,1,0:T(8,128)(2,1)}, u32[]{:S(2)}, u32[]{:S(2)}) collective-permute-start(bf16[8,2,32,256]{3,2,1,0:T(8,128)(2,1)S(1)} %all-to-all-done.refs_8_), channel_id=1, source_target_pairs={{0,192},{8,200},{16,208},{24,216},{32,224},{40,232},{48,240},{56,2... | collective-permute-start | bytes 786440 | tf_op jit(solution)/shard_map/ppermute | solution.py:164
  38.2 4.1 %all-to-all-start.1 = ((bf16[8,2,32,256]{3,2,1,0:T(8,128)(2,1)}), bf16[8,2,32,256]{3,2,1,0:T(8,128)(2,1)}, u32[]{:S(2)}, u32[]{:S(2)}) async-start(bf16[8,2,32,256]{3,2,1,0:T(8,128)(2,1)} %get-tuple-element.5), calls=%async_computation.1 | async-start | bytes 524288 | tf_op jit(solution)/shard_map/all_to_all | solution.py:160
  42.3 4.2 %collective-permute-done.7.refs_9_ = bf16[8,2,32,256]{3,2,1,0:T(8,128)(2,1)} collective-permute-done((bf16[8,2,32,256]{3,2,1,0:T(8,128)(2,1)S(1)}, bf16[8,2,32,256]{3,2,1,0:T(8,128)(2,1)}, u32[]{:S(2)}, u32[]{:S(2)}) %collective-permute-start.7) | collective-permute-done | bytes 262176 | tf_op jit(solution)/shard_map/ppermute | solution.py:164
  46.5 0.9 %copy-done.3 = bf16[8,2,32,256]{3,2,1,0:T(8,128)(2,1)S(1)} copy-done((bf16[8,2,32,256]{3,2,1,0:T(8,128)(2,1)S(1)}, bf16[8,2,32,256]{3,2,1,0:T(8,128)(2,1)}, u32[]{:S(2)}) %copy-start.3) | copy-done | bytes 262168
  47.5 4.0 %shard_map.48 = bf16[2,1024,128]{2,1,0:T(8,128)(2,1)} custom-call(s32[4]{0:T(128)S(1)} %pad_add_fusion.at_ref, bf16[2,1024,128]{2,1,0:T(8,128)(2,1)S(1)} %copy-done, bf16[2,1024,128]{2,1,0:T(8,128)(2,1)S(1)} %collective-permute-done.refs_1_.refs_3_, bf16[2,1024,128]{2,1,0:T(8,128)(2,1)S(1)} %collective-permute-done.1.refs_2_.refs_4_, ...), custom_call_target="tpu_custom_call" | custom-call | flops 1073741824 | bytes 6291456 | tf_op jit(solution)/shard_map/pallas_call | solution.py:105
  51.5 0.6 collective-permute-start.10
  52.0 0.7 %all-to-all-done.1.refs_10_ = bf16[8,2,32,256]{3,2,1,0:T(8,128)(2,1)} async-done(((bf16[8,2,32,256]{3,2,1,0:T(8,128)(2,1)}), bf16[8,2,32,256]{3,2,1,0:T(8,128)(2,1)}, u32[]{:S(2)}, u32[]{:S(2)}) %all-to-all-start.1) | async-done | bytes 262176 | tf_op jit(solution)/shard_map/all_to_all | solution.py:160
  52.7 0.3 collective-permute-start.13
  53.0 4.9 %collective-permute-start.12 = (bf16[8,2,32,256]{3,2,1,0:T(8,128)(2,1)}, bf16[8,2,32,256]{3,2,1,0:T(8,128)(2,1)}, u32[]{:S(2)}, u32[]{:S(2)}) collective-permute-start(bf16[8,2,32,256]{3,2,1,0:T(8,128)(2,1)} %all-to-all-done.1.refs_10_), channel_id=1, source_target_pairs={{0,128},{8,136},{16,144},{24,152},{32,160},{40,168},{48,176},{56,1... | collective-permute-start | bytes 786440 | tf_op jit(solution)/shard_map/ppermute | solution.py:164
  57.9 1.0 %constant_dynamic-slice_fusion.rows_ref = bf16[128,1024]{1,0:T(8,128)(2,1)S(1)} fusion(bf16[1024,1024]{1,0:T(8,128)(2,1)} %fock_ref.1, s32[]{:T(128)S(6)} %select_n.25), kind=kLoop, calls=%fused_computation.3 | loop fusion | bytes 524292 | tf_op jit(solution)/shard_map/dynamic_slice | solution.py:176
  58.8 1.6 %copy-done.1 = bf16[1024,1024]{1,0:T(8,128)(2,1)S(1)} copy-done((bf16[1024,1024]{1,0:T(8,128)(2,1)S(1)}, bf16[1024,1024]{1,0:T(8,128)(2,1)}, u32[]{:S(2)}) %copy-start.1) | copy-done | bytes 2097176
  60.4 3.6 %shard_map.46.refs_0_ = f32[2,1024,128]{2,1,0:T(8,128)S(1)} custom-call(s32[4]{0:T(128)S(1)} %pad_add_fusion.at_ref, bf16[1024,1024]{1,0:T(8,128)(2,1)S(1)} %copy-done.1, bf16[128,1024]{1,0:T(8,128)(2,1)S(1)} %constant_dynamic-slice_fusion.rows_ref, bf16[2,1024,128]{2,1,0:T(8,128)(2,1)S(1)} %copy-done, ...), custom_call_target="tpu_custom_call" | custom-call | flops 1073741824 | bytes 4194304 | tf_op jit(solution)/shard_map/pallas_call | solution.py:57
  64.0 0.6 collective-permute-done.12.refs_12_
  64.6 2.4 %collective-permute-done.11.refs_11_ = bf16[8,2,32,256]{3,2,1,0:T(8,128)(2,1)} collective-permute-done((bf16[8,2,32,256]{3,2,1,0:T(8,128)(2,1)}, bf16[8,2,32,256]{3,2,1,0:T(8,128)(2,1)}, u32[]{:S(2)}, u32[]{:S(2)}) %collective-permute-start.11) | collective-permute-done | bytes 262176 | tf_op jit(solution)/shard_map/ppermute | solution.py:164
  67.0 4.3 %shard_map.49 = bf16[2,1024,128]{2,1,0:T(8,128)(2,1)} custom-call(s32[4]{0:T(128)S(1)} %pad_add_fusion.at_ref, f32[2,1024,128]{2,1,0:T(8,128)S(1)} %shard_map.46.refs_0_, bf16[2,1024,128]{2,1,0:T(8,128)(2,1)} %collective-permute-done.10.refs_1_, bf16[2,1024,128]{2,1,0:T(8,128)(2,1)S(1)} %copy-done, ...), custom_call_target="tpu_custom_call" | custom-call | flops 1073741824 | bytes 6291456 | tf_op jit(solution)/shard_map/pallas_call | solution.py:105
  (19 shorter events, 0.0 us)
Async XLA Ops:
  0.0 17.5 %copy-start = (bf16[2,1024,128]{2,1,0:T(8,128)(2,1)S(1)}, bf16[2,1024,128]{2,1,0:T(8,128)(2,1)}, u32[]{:S(2)}) copy-start(bf16[2,1024,128]{2,1,0:T(8,128)(2,1)} %refs_2_.1) | copy-start | bytes 1572868
  0.0 30.1 %collective-permute-start.5 = (bf16[2,1024,128]{2,1,0:T(8,128)(2,1)}, bf16[2,1024,128]{2,1,0:T(8,128)(2,1)S(1)}, u32[]{:S(2)}, u32[]{:S(2)}) collective-permute-start(bf16[2,1024,128]{2,1,0:T(8,128)(2,1)} %refs_2_.1), channel_id=1, source_target_pairs={{0,2},{1,3},{2,4},{3,5},{4,6},{5,7},{6,0},{7,1},{8,10},{9,11},{10,... | collective-permute-start | bytes 1572872 | tf_op jit(solution)/shard_map/ppermute | solution.py:173
  1.5 28.7 %collective-permute-start.3 = (bf16[2,1024,128]{2,1,0:T(8,128)(2,1)}, bf16[2,1024,128]{2,1,0:T(8,128)(2,1)S(1)}, u32[]{:S(2)}, u32[]{:S(2)}) collective-permute-start(bf16[2,1024,128]{2,1,0:T(8,128)(2,1)} %refs_2_.1), channel_id=1, source_target_pairs={{0,4},{1,5},{2,6},{3,7},{4,0},{5,1},{6,2},{7,3},{8,12},{9,13},{10,... | collective-permute-start | bytes 1572872 | tf_op jit(solution)/shard_map/ppermute | solution.py:173
  4.2 26.4 %collective-permute-start.1 = (bf16[2,1024,128]{2,1,0:T(8,128)(2,1)}, bf16[2,1024,128]{2,1,0:T(8,128)(2,1)S(1)}, u32[]{:S(2)}, u32[]{:S(2)}) collective-permute-start(bf16[2,1024,128]{2,1,0:T(8,128)(2,1)} %refs_2_.1), channel_id=1, source_target_pairs={{0,6},{1,7},{2,0},{3,1},{4,2},{5,3},{6,4},{7,5},{8,14},{9,15},{10,... | collective-permute-start | bytes 1572872 | tf_op jit(solution)/shard_map/ppermute | solution.py:173
  5.7 0.9 %copy-start.4 = (bf16[4,32,4,128]{3,2,1,0:T(4,128)(2,1)S(1)}, bf16[4,32,4,128]{3,2,1,0:T(4,128)(2,1)}, u32[]{:S(2)}) copy-start(bf16[4,32,4,128]{3,2,1,0:T(4,128)(2,1)} %ints_ref.1) | copy-start | bytes 393220
  6.6 0.7 copy-start.5
  9.1 19.5 %all-to-all-start = ((bf16[8,2,32,256]{3,2,1,0:T(8,128)(2,1)}), bf16[8,2,32,256]{3,2,1,0:T(8,128)(2,1)S(1)}, u32[]{:S(2)}, u32[]{:S(2)}) async-start(bf16[8,2,32,256]{3,2,1,0:T(8,128)(2,1)} %get-tuple-element.6), calls=%async_computation | async-start | bytes 524288 | tf_op jit(solution)/shard_map/all_to_all | solution.py:160
  17.5 13.2 %collective-permute-start = (bf16[2,1024,128]{2,1,0:T(8,128)(2,1)S(1)}, bf16[2,1024,128]{2,1,0:T(8,128)(2,1)S(1)}, u32[]{:S(2)}, u32[]{:S(2)}) collective-permute-start(bf16[2,1024,128]{2,1,0:T(8,128)(2,1)S(1)} %copy-done), channel_id=1, source_target_pairs={{0,1},{1,0},{2,3},{3,2},{4,5},{5,4},{6,7},{7,6},{8,9},{9,8},{10,11... | collective-permute-start | bytes 1572872 | tf_op jit(solution)/shard_map/ppermute | solution.py:156
  28.6 6.4 %collective-permute-start.9 = (bf16[8,2,32,256]{3,2,1,0:T(8,128)(2,1)S(1)}, bf16[8,2,32,256]{3,2,1,0:T(8,128)(2,1)S(1)}, u32[]{:S(2)}, u32[]{:S(2)}) collective-permute-start(bf16[8,2,32,256]{3,2,1,0:T(8,128)(2,1)S(1)} %all-to-all-done.refs_8_), channel_id=1, source_target_pairs={{0,64},{8,72},{16,80},{24,88},{32,96},{40,104},{48,112},{56,120},{... | collective-permute-start | bytes 786440 | tf_op jit(solution)/shard_map/ppermute | solution.py:164
  30.2 16.4 %collective-permute-start.6 = (bf16[2,1024,128]{2,1,0:T(8,128)(2,1)S(1)}, bf16[2,1024,128]{2,1,0:T(8,128)(2,1)S(1)}, u32[]{:S(2)}, u32[]{:S(2)}) collective-permute-start(bf16[2,1024,128]{2,1,0:T(8,128)(2,1)S(1)} %collective-permute-done.5.refs_6_.refs_8_), channel_id=1, source_target_pairs={{0,1},{1,0},{2,3},{3,2},{4,5},{5,4},{6,7},{7,6},{8,9},{9,8},{10,11... | collective-permute-start | bytes 1572872 | tf_op jit(solution)/shard_map/ppermute | solution.py:156
  30.2 16.3 %collective-permute-start.4 = (bf16[2,1024,128]{2,1,0:T(8,128)(2,1)S(1)}, bf16[2,1024,128]{2,1,0:T(8,128)(2,1)}, u32[]{:S(2)}, u32[]{:S(2)}) collective-permute-start(bf16[2,1024,128]{2,1,0:T(8,128)(2,1)S(1)} %collective-permute-done.3.refs_4_.refs_6_), channel_id=1, source_target_pairs={{0,1},{1,0},{2,3},{3,2},{4,5},{5,4},{6,7},{7,6},{8,9},{9,8},{10,11... | collective-permute-start | bytes 1572872 | tf_op jit(solution)/shard_map/ppermute | solution.py:156
  30.7 15.8 %collective-permute-start.2 = (bf16[2,1024,128]{2,1,0:T(8,128)(2,1)S(1)}, bf16[2,1024,128]{2,1,0:T(8,128)(2,1)}, u32[]{:S(2)}, u32[]{:S(2)}) collective-permute-start(bf16[2,1024,128]{2,1,0:T(8,128)(2,1)S(1)} %collective-permute-done.1.refs_2_.refs_4_), channel_id=1, source_target_pairs={{0,1},{1,0},{2,3},{3,2},{4,5},{5,4},{6,7},{7,6},{8,9},{9,8},{10,11... | collective-permute-start | bytes 1572872 | tf_op jit(solution)/shard_map/ppermute | solution.py:156
  30.8 11.5 %collective-permute-start.8 = (bf16[8,2,32,256]{3,2,1,0:T(8,128)(2,1)S(1)}, bf16[8,2,32,256]{3,2,1,0:T(8,128)(2,1)}, u32[]{:S(2)}, u32[]{:S(2)}) collective-permute-start(bf16[8,2,32,256]{3,2,1,0:T(8,128)(2,1)S(1)} %all-to-all-done.refs_8_), channel_id=1, source_target_pairs={{0,128},{8,136},{16,144},{24,152},{32,160},{40,168},{48,176},{56,1... | collective-permute-start | bytes 786440 | tf_op jit(solution)/shard_map/ppermute | solution.py:164
  34.9 0.7 copy-start.2
  35.6 10.9 %collective-permute-start.7 = (bf16[8,2,32,256]{3,2,1,0:T(8,128)(2,1)S(1)}, bf16[8,2,32,256]{3,2,1,0:T(8,128)(2,1)}, u32[]{:S(2)}, u32[]{:S(2)}) collective-permute-start(bf16[8,2,32,256]{3,2,1,0:T(8,128)(2,1)S(1)} %all-to-all-done.refs_8_), channel_id=1, source_target_pairs={{0,192},{8,200},{16,208},{24,216},{32,224},{40,232},{48,240},{56,2... | collective-permute-start | bytes 786440 | tf_op jit(solution)/shard_map/ppermute | solution.py:164
  38.2 14.5 %all-to-all-start.1 = ((bf16[8,2,32,256]{3,2,1,0:T(8,128)(2,1)}), bf16[8,2,32,256]{3,2,1,0:T(8,128)(2,1)}, u32[]{:S(2)}, u32[]{:S(2)}) async-start(bf16[8,2,32,256]{3,2,1,0:T(8,128)(2,1)} %get-tuple-element.5), calls=%async_computation.1 | async-start | bytes 524288 | tf_op jit(solution)/shard_map/all_to_all | solution.py:160
  46.5 1.0 %copy-start.3 = (bf16[8,2,32,256]{3,2,1,0:T(8,128)(2,1)S(1)}, bf16[8,2,32,256]{3,2,1,0:T(8,128)(2,1)}, u32[]{:S(2)}) copy-start(bf16[8,2,32,256]{3,2,1,0:T(8,128)(2,1)} %copy-done.2) | copy-start | bytes 786436
  51.5 15.5 %collective-permute-start.10 = (bf16[2,1024,128]{2,1,0:T(8,128)(2,1)}, bf16[2,1024,128]{2,1,0:T(8,128)(2,1)}, u32[]{:S(2)}, u32[]{:S(2)}) collective-permute-start(bf16[2,1024,128]{2,1,0:T(8,128)(2,1)} %shard_map.48), channel_id=1, source_target_pairs={{0,8},{8,0},{16,24},{24,16},{32,40},{40,32},{48,56},{56,48},{64,72... | collective-permute-start | bytes 1572872 | tf_op jit(solution)/shard_map/ppermute | solution.py:179
  52.7 11.3 %collective-permute-start.13 = (bf16[8,2,32,256]{3,2,1,0:T(8,128)(2,1)}, bf16[8,2,32,256]{3,2,1,0:T(8,128)(2,1)S(1)}, u32[]{:S(2)}, u32[]{:S(2)}) collective-permute-start(bf16[8,2,32,256]{3,2,1,0:T(8,128)(2,1)} %all-to-all-done.1.refs_10_), channel_id=1, source_target_pairs={{0,64},{8,72},{16,80},{24,88},{32,96},{40,104},{48,112},{56,120},{... | collective-permute-start | bytes 786440 | tf_op jit(solution)/shard_map/ppermute | solution.py:164
  53.0 11.6 %collective-permute-start.12 = (bf16[8,2,32,256]{3,2,1,0:T(8,128)(2,1)}, bf16[8,2,32,256]{3,2,1,0:T(8,128)(2,1)}, u32[]{:S(2)}, u32[]{:S(2)}) collective-permute-start(bf16[8,2,32,256]{3,2,1,0:T(8,128)(2,1)} %all-to-all-done.1.refs_10_), channel_id=1, source_target_pairs={{0,128},{8,136},{16,144},{24,152},{32,160},{40,168},{48,176},{56,1... | collective-permute-start | bytes 786440 | tf_op jit(solution)/shard_map/ppermute | solution.py:164
  57.9 9.1 %collective-permute-start.11 = (bf16[8,2,32,256]{3,2,1,0:T(8,128)(2,1)}, bf16[8,2,32,256]{3,2,1,0:T(8,128)(2,1)}, u32[]{:S(2)}, u32[]{:S(2)}) collective-permute-start(bf16[8,2,32,256]{3,2,1,0:T(8,128)(2,1)} %all-to-all-done.1.refs_10_), channel_id=1, source_target_pairs={{0,192},{8,200},{16,208},{24,216},{32,224},{40,232},{48,240},{56,2... | collective-permute-start | bytes 786440 | tf_op jit(solution)/shard_map/ppermute | solution.py:164
  58.8 1.6 %copy-start.1 = (bf16[1024,1024]{1,0:T(8,128)(2,1)S(1)}, bf16[1024,1024]{1,0:T(8,128)(2,1)}, u32[]{:S(2)}) copy-start(bf16[1024,1024]{1,0:T(8,128)(2,1)} %fock_ref.1) | copy-start | bytes 6291460

commit v3 on v2

--- a/solution.py
+++ b/solution.py
@@ -14,23 +14,30 @@
 CORES = [(q, q ^ 1) for q in range(2 * NX)]
 X_GROUPS = [[2 * x + c for x in range(NX)] for c in range(2)]
 Y_GROUPS = [[y * NZ + z for y in range(NY)] for z in range(NZ)]
-Z_GROUPS = [[y * NZ + z for z in range(NZ)] for y in range(NY)]
+Z_RING = lambda d: [(y * NZ + z, y * NZ + (z + d) % NZ) for y in range(NY) for z in range(NZ)]
 ROWS = 256
 MIB = 1 << 20
 
 
 VM = 16
-COST = 1
+COST = 8
+CROWS = 1024
+CHUNKS = 4
+MINE_COST = 8
 
 
 VMEM = pl.BlockSpec(memory_space=pltpu.VMEM)
 SMEM = pl.BlockSpec(memory_space=pltpu.SMEM)
 
 
+def blocks_of(refs):
+    return [ref.at[d] for d in range(NX) for ref in refs]
+
+
 def fock_kernel(at_ref, fock_ref, rows_ref, *refs):
     amps, out_ref = refs[:-1], refs[-1]
-    x, core = at_ref[2], at_ref[3]
-    own = amps[0]
+    x, core = 0, at_ref[3]
+    own, amps = amps[0], blocks_of(amps[1:])
     width = own.shape[2]
     both = jnp.concatenate([own[0], own[1]], axis=1)
     fock = []
@@ -61,60 +68,79 @@
         out_specs=VMEM,
         compiler_params=pltpu.CompilerParams(vmem_limit_bytes=VM * MIB),
         cost_estimate=pl.CostEstimate(
-            flops=2 * pairs * width * width * cols * 2, bytes_accessed=4 * MIB, transcendentals=0
+            flops=1 * 4 * pairs * width * width * cols, bytes_accessed=4 * MIB, transcendentals=0
         ),
     )(at, fock_vv, fock_rows, *amps)
 
 
-def cycle_kernel(last, at_ref, *refs):
-    fock_ref = sent_ref = None
-    if last:
-        fock_ref, sent_ref, refs = refs[0], refs[1], refs[2:]
+def cycle_kernel(at_ref, *refs):
     held, out_ref, refs = refs[-1], refs[-2], refs[:-2]
     ints, amps = refs[-NY:], refs[:-NY]
-    y, x, core = at_ref[0], at_ref[2], at_ref[3]
+    y, z, core = at_ref[0], at_ref[1], at_ref[3]
+    amps = blocks_of(amps)
     n_z, pairs, depth, cols = ints[0].shape
-    side, width = n_z // 2, cols // 2
+    width = cols // 2
     for e in range(NY):
-        d = lax.rem(y + e - x + 2 * NX, NX)
-        for s in range(2):
-            c = 1 - core if s else core
+        chip = lax.rem(y + e, NY)
+        for g in range(n_z // 2):
+            place = lax.rem(z // 2 + g, n_z // 2)
+            s = lax.rem(place // 2 + core, 2)
             for p in range(pairs):
-                part = ints[e][pl.ds(c * side, side), p]
-                held[d, s, p] = part.reshape(side * depth, cols)
+                part = ints[e][2 * g : 2 * g + 2, p]
+                held[chip, s, p, lax.rem(place, 2)] = part.reshape(2 * depth, cols)
     rhs = jnp.concatenate(
-        [held[i // 2, i % 2, p] for p in range(pairs) for i in range(len(amps))], axis=0
+        [held[i // 2, i % 2, p].reshape(n_z // 2 * depth, cols) for p in range(pairs) for i in range(len(amps))], axis=0
     )
 
-    @pl.loop(0, out_ref.shape[1] // ROWS)
+    @pl.loop(0, out_ref.shape[1] // CROWS)
     def _(r):
-        at = pl.ds(pl.multiple_of(r * ROWS, ROWS), ROWS)
+        at = pl.ds(pl.multiple_of(r * CROWS, CROWS), CROWS)
         lhs = jnp.concatenate([a[p, at, :] for p in range(pairs) for a in amps], axis=1)
         total = jnp.dot(lhs, rhs, preferred_element_type=jnp.float32)
         for p in range(pairs):
-            mine_p = total[:, p * width : (p + 1) * width]
-            if last:
-                mine_p = mine_p + sent_ref[p, at, :].astype(jnp.float32)
-                mine_p = mine_p.astype(jnp.bfloat16).astype(jnp.float32) + fock_ref[p, at, :]
-            out_ref[p, at, :] = mine_p.astype(out_ref.dtype)
-
-
-def cycle_sum(at, before, amps, ints, shape, cost):
+            out_ref[p, at, :] = total[:, p * width : (p + 1) * width].astype(out_ref.dtype)
+
+
+def cycle_sum(at, amps, ints, dtype, cost):
     n_z, pairs, depth, cols = ints[0].shape
-    last = bool(before)
-    return pl.pallas_call(
-        functools.partial(cycle_kernel, last),
-        out_shape=jax.ShapeDtypeStruct(shape, jnp.bfloat16),
-        in_specs=[SMEM] + [VMEM] * (len(before) + len(amps) + len(ints)),
+    shape = amps[0].shape[1:]
+    return pl.pallas_call(
+        cycle_kernel,
+        out_shape=jax.ShapeDtypeStruct(shape, dtype),
+        in_specs=[SMEM] + [VMEM] * (len(amps) + len(ints)),
         out_specs=VMEM,
-        scratch_shapes=[pltpu.VMEM((NY, 2, pairs, n_z // 2 * depth, cols), jnp.bfloat16)],
+        scratch_shapes=[pltpu.VMEM((NY, 2, pairs, 2, 2 * depth, cols), jnp.bfloat16)],
         compiler_params=pltpu.CompilerParams(vmem_limit_bytes=VM * MIB),
         cost_estimate=pl.CostEstimate(
             flops=cost * shape[0] * shape[1] * shape[1] * shape[2] * 4,
             bytes_accessed=6 * MIB,
             transcendentals=0,
         ),
-    )(at, *before, *amps, *ints)
+    )(at, *amps, *ints)
+
+
+def add_kernel(fock_ref, mine_ref, sent_ref, out_ref, done, sems):
+    rows = out_ref.shape[1] // CHUNKS
+    copies = []
+    for i in range(CHUNKS):
+        at = pl.ds(i * rows, rows)
+        cycle = (mine_ref[:, at, :] + sent_ref[:, at, :].astype(jnp.float32)).astype(jnp.bfloat16)
+        done[:, at, :] = (fock_ref[:, at, :] + cycle.astype(jnp.float32)).astype(jnp.bfloat16)
+        copies.append(pltpu.make_async_copy(done.at[:, at, :], out_ref.at[:, at, :], sems.at[i]))
+        copies[-1].start()
+    for copy in copies:
+        copy.wait()
+
+
+def add(fock_part, mine, sent):
+    return pl.pallas_call(
+        add_kernel,
+        out_shape=jax.ShapeDtypeStruct(sent.shape, jnp.bfloat16),
+        in_specs=[VMEM] * 3,
+        out_specs=pl.BlockSpec(memory_space=pl.ANY),
+        scratch_shapes=[pltpu.VMEM(sent.shape, jnp.bfloat16), pltpu.SemaphoreType.DMA((CHUNKS,))],
+        compiler_params=pltpu.CompilerParams(vmem_limit_bytes=VM * MIB),
+    )(fock_part, mine, sent)
 
 
 def prepare_kernel(at_ref, mask_ref, ints_ref, out_ref):
@@ -131,14 +157,13 @@
         for j in range(2):
             pair = [ints_ref[k, :, 2 * j + p, :] * keep for p in range(2)]
             pair = jnp.concatenate(pair, axis=1)
-            part = int(j == k // 2)
-            for z in range(k // 2, NZ, 2):
-                out_ref[part, z, k % 2] = pair
+            to = lax.rem(at_ref[1] + k // 2, 2)
+            out_ref[to, int(j == k // 2), k % 2] = pair
 
 
 def prepare(at, tile_mask, cycle_ints):
     occ, depth, _, cols = cycle_ints.shape
-    shape = (2, NZ, occ // 2, depth, 2 * cols)
+    shape = (2, 2, occ // 2, depth, 2 * cols)
     return pl.pallas_call(
         prepare_kernel,
         out_shape=jax.ShapeDtypeStruct(shape, jnp.bfloat16),
@@ -156,8 +181,21 @@
     return lax.ppermute(a, "ints", CORES)
 
 
-def along_z(a):
-    return lax.all_to_all(a, "amp", 0, 0, tiled=True, axis_index_groups=Z_GROUPS)
+def pair_along_z(halves, z):
+    got = lax.ppermute(halves[1], "amp", Z_PAIR)
+    first = jnp.where(z % 2 == 0, halves[0], got)
+    second = jnp.where(z % 2 == 0, got, halves[0])
+    return jnp.stack([first, second], axis=1)
+
+
+def along_z(pair):
+    parts = [pair] + [lax.ppermute(pair, "amp", Z_RING(-2 * g)) for g in (1, 2, 3)]
+    return [jnp.concatenate([part[r] for part in parts], axis=0) for r in range(2)]
+
+
+def spread(a, axis, groups):
+    a = jnp.broadcast_to(a[None], (len(groups[0]),) + a.shape)
+    return lax.all_to_all(a, axis, 0, 0, axis_index_groups=groups)
 
 
 def along_y(row):
@@ -167,17 +205,18 @@
 def body(amplitudes, fock_vv, cycle_ints, tile_mask):
     amp, ints = lax.axis_index("amp"), lax.axis_index("ints")
     at = jnp.stack([amp // NZ, amp % NZ, ints // 2, ints % 2]).astype(jnp.int32)
-    to_z = prepare(at, tile_mask, cycle_ints)
-    rows = [along_z(to_z[0]), along_z(to_z[1])]
+    halves = prepare(at, tile_mask, cycle_ints)
+    rows = along_z(pair_along_z(halves, at[1]))
+    gathered = spread(amplitudes, "ints", X_GROUPS)
+    gathered, *rows = lax.optimization_barrier((gathered, *rows))
     partners, mine = along_y(rows[0]), along_y(rows[1])
-    own = [amplitudes] + [lax.ppermute(amplitudes, "ints", X_RING(-d)) for d in (1, 2, 3)]
-    own = [b for a in own for b in (a, swap(a))]
+    own = [gathered, swap(gathered)]
 
     fock_rows = lax.dynamic_slice_in_dim(fock_vv, ints * amplitudes.shape[2], amplitudes.shape[2], 0)
-    fock_part = fock_terms(at, fock_vv, fock_rows, own)
-    sent = cycle_sum(at, [], own, partners, amplitudes.shape, COST)
+    fock_part = fock_terms(at, fock_vv, fock_rows, [amplitudes, *own])
+    sent = cycle_sum(at, own, partners, jnp.bfloat16, COST)
     sent = lax.ppermute(sent, "amp", Z_PAIR)
-    return cycle_sum(at, [fock_part, sent], own, mine, amplitudes.shape, 1)
+    return add(fock_part, cycle_sum(at, own, mine, jnp.float32, MINE_COST), sent)
 
 
 def solution(mesh):

time: 71.8 us -> 68.4 us (0.953)
  local copies, waits for them, and re-layouts: 6.64 us -> 3.66 us
  waiting for transfers between devices: 22.1 us -> 23.8 us
  Pallas kernels: 12.8 us -> 11.7 us
  starting transfers between devices: 29.6 us -> 28.6 us
    ppermute x3 -> x4, waiting for transfers between devices: 0.01 us -> 10.7 us  [the longest x3 8.39 us: along_z(): lax.ppermute(pair, 'amp', Z_RING(-2 * g))]
    all_to_all x2 -> x1, waiting for transfers between devices: 11.6 us -> 2.21 us  [spread(): return lax.all_to_all(a, axis, 0, 0, axis_index_groups=groups)]
    all_to_all x2 -> x1, starting transfers between devices: 12.5 us -> 4.42 us  [spread(): return lax.all_to_all(a, axis, 0, 0, axis_index_groups=groups)]
    ppermute x3 -> x4, starting transfers between devices: 5.65 us -> 12.2 us  [the longest x3 10.2 us: along_z(): lax.ppermute(pair, 'amp', Z_RING(-2 * g))]
    unnamed x12 -> x8, local copies, waits for them, and re-layouts: 4.84 us -> 0.02 us
    ppermute x1, waiting for transfers between devices: 0.01 us -> 3.17 us  [body(): sent = lax.ppermute(sent, 'amp', Z_PAIR)]
    ppermute x6, waiting for transfers between devices: 10.4 us -> 7.66 us  [along_y(): return [row] + [lax.ppermute(row, 'amp', Y_RING(-e)) for e in (1, 2, 3)]]
    broadcast_in_dim x0 -> x1, local copies, waits for them, and re-layouts: none -> 2.64 us  [spread(): a = jnp.broadcast_to(a[None], (len(groups[0]),) + a.shape)]
  transfers between devices with their start and end apart: 16 -> 13, of which waited for: 6 -> 7; matrix products, arithmetic and copies ran while one was open for 3% -> 2% of each run, Pallas kernels for 12% -> 16%
where the time goes in v3:
time: 68.4 us; the launch traced here: 68.1 us
  starting transfers between devices  28.6 us (42%)
  waiting for transfers between devices  23.8 us (35%)
  Pallas kernels  11.7 us (17%)
  local copies, waits for them, and re-layouts  3.66 us (5%)
    ppermute x3, starting transfers between devices, along_z(): lax.ppermute(pair, 'amp', Z_RING(-2 * g))  10.2 us
    ppermute x6, starting transfers between devices, along_y(): return [row] + [lax.ppermute(row, 'amp', Y_RING(-e)) for e in (1, 2, 3)]  9.99 us
    ppermute x3, waiting for transfers between devices, along_z(): lax.ppermute(pair, 'amp', Z_RING(-2 * g))  8.39 us
    ppermute x6, waiting for transfers between devices, along_y(): return [row] + [lax.ppermute(row, 'amp', Y_RING(-e)) for e in (1, 2, 3)]  7.66 us
    pallas_call x2, Pallas kernels, cycle_sum(): pl.pallas_call(cycle_kernel, out_shape=jax.ShapeDtypeStruct(shape, dtype)...  5.91 us
    all_to_all x1, starting transfers between devices, spread(): return lax.all_to_all(a, axis, 0, 0, axis_index_groups=groups)  4.42 us
    pallas_call x1, Pallas kernels, fock_terms(): pl.pallas_call(fock_kernel, out_shape=jax.ShapeDtypeStruct((pairs, width,...  4.01 us
    ppermute x1, waiting for transfers between devices, body(): sent = lax.ppermute(sent, 'amp', Z_PAIR)  3.17 us
  transfers between devices with their start and end apart: 13, of which 7 were waited for; matrix products, arithmetic and copies ran while one was open for 2% of the time, Pallas kernels for 16%

profile of v3, /device:TPU:8, one launch (start us, length us, event | category | flops | bytes accessed | tf_op | source)
XLA Modules:
  0.0 68.1 jit_solution(10815106822911056867)
XLA Ops:
  0.0 2.6 %broadcast_in_dim.2 = bf16[4,2,1024,128]{3,2,1,0:T(8,128)(2,1)} broadcast(bf16[2,1024,128]{2,1,0:T(8,128)(2,1)} %refs_0_.1), dimensions={1,2,3} | broadcast | bytes 2621440 | tf_op jit(solution)/shard_map/broadcast_in_dim | solution.py:197
  2.6 4.4 %all-to-all-start = ((bf16[4,2,1024,128]{3,2,1,0:T(8,128)(2,1)}), bf16[4,2,1024,128]{3,2,1,0:T(8,128)(2,1)S(1)}, u32[]{:S(2)}, u32[]{:S(2)}) async-start(bf16[4,2,1024,128]{3,2,1,0:T(8,128)(2,1)} %broadcast_in_dim.2), calls=%async_computation | async-start | bytes 4194304 | tf_op jit(solution)/shard_map/all_to_all | solution.py:198
  7.1 0.1 pad_add_fusion.at_ref
  7.1 0.9 %shard_map.46 = bf16[2,2,2,32,256]{4,3,2,1,0:T(8,128)(2,1)S(1)} custom-call(s32[4]{0:T(128)S(1)} %pad_add_fusion.at_ref, s32[16,16]{1,0:T(8,128)S(1)} %copy-done.3, bf16[4,32,4,128]{3,2,1,0:T(4,128)(2,1)S(1)} %copy-done.2), custom_call_target="tpu_custom_call" | custom-call | tf_op jit(solution)/shard_map/pallas_call | solution.py:167
  8.1 2.0 %collective-permute-start = (bf16[2,2,32,256]{3,2,1,0:T(8,128)(2,1)S(1)}, bf16[2,2,32,256]{3,2,1,0:T(8,128)(2,1)S(1)}, u32[]{:S(2)}, u32[]{:S(2)}) collective-permute-start(bf16[2,2,32,256]{3,2,1,0:T(8,128)(2,1)S(1)} %slice_bitcast_fusion.6), channel_id=1, source_target_pairs={{0,8},{8,0},{16,24},{24,16},{32,40},{40,32},{48,56},{56,48},{64,72... | collective-permute-start | bytes 196616 | tf_op jit(solution)/shard_map/ppermute | solution.py:185
  10.1 2.3 %collective-permute-done = bf16[2,2,32,256]{3,2,1,0:T(8,128)(2,1)S(1)} collective-permute-done((bf16[2,2,32,256]{3,2,1,0:T(8,128)(2,1)S(1)}, bf16[2,2,32,256]{3,2,1,0:T(8,128)(2,1)S(1)}, u32[]{:S(2)}, u32[]{:S(2)}) %collective-permute-start) | collective-permute-done | bytes 65568 | tf_op jit(solution)/shard_map/ppermute | solution.py:185
  12.5 7.3 %collective-permute-start.2 = (bf16[2,2,2,32,256]{4,3,2,1,0:T(8,128)(2,1)S(1)}, bf16[2,2,2,32,256]{4,3,2,1,0:T(8,128)(2,1)S(1)}, u32[]{:S(2)}, u32[]{:S(2)}) collective-permute-start(bf16[2,2,2,32,256]{4,3,2,1,0:T(8,128)(2,1)S(1)} %pad_maximum_fusion.2), channel_id=1, source_target_pairs={{0,32},{8,40},{16,48},{24,56},{32,0},{40,8},{48,16},{56,24},{64,96... | collective-permute-start | bytes 393224 | tf_op jit(solution)/shard_map/ppermute | solution.py:192
  19.7 0.0 collective-permute-start.1
  19.7 2.9 %collective-permute-start.3 = (bf16[2,2,2,32,256]{4,3,2,1,0:T(8,128)(2,1)S(1)}, bf16[2,2,2,32,256]{4,3,2,1,0:T(8,128)(2,1)S(1)}, u32[]{:S(2)}, u32[]{:S(2)}) collective-permute-start(bf16[2,2,2,32,256]{4,3,2,1,0:T(8,128)(2,1)S(1)} %pad_maximum_fusion.2), channel_id=1, source_target_pairs={{0,16},{8,24},{16,32},{24,40},{32,48},{40,56},{48,0},{56,8},{64,80... | collective-permute-start | bytes 393224 | tf_op jit(solution)/shard_map/ppermute | solution.py:192
  22.7 2.8 %collective-permute-done.2 = bf16[2,2,2,32,256]{4,3,2,1,0:T(8,128)(2,1)S(1)} collective-permute-done((bf16[2,2,2,32,256]{4,3,2,1,0:T(8,128)(2,1)S(1)}, bf16[2,2,2,32,256]{4,3,2,1,0:T(8,128)(2,1)S(1)}, u32[]{:S(2)}, u32[]{:S(2)}) %collective-permute-start.2) | collective-permute-done | bytes 131104 | tf_op jit(solution)/shard_map/ppermute | solution.py:192
  25.5 5.6 %collective-permute-done.1 = bf16[2,2,2,32,256]{4,3,2,1,0:T(8,128)(2,1)S(1)} collective-permute-done((bf16[2,2,2,32,256]{4,3,2,1,0:T(8,128)(2,1)S(1)}, bf16[2,2,2,32,256]{4,3,2,1,0:T(8,128)(2,1)S(1)}, u32[]{:S(2)}, u32[]{:S(2)}) %collective-permute-start.1) | collective-permute-done | bytes 131104 | tf_op jit(solution)/shard_map/ppermute | solution.py:192
  31.1 0.0 collective-permute-done.3
  31.1 0.1 pad_maximum_fusion
  31.2 2.2 %all-to-all-done.refs_1_.refs_0_ = bf16[4,2,1024,128]{3,2,1,0:T(8,128)(2,1)S(1)} async-done(((bf16[4,2,1024,128]{3,2,1,0:T(8,128)(2,1)}), bf16[4,2,1024,128]{3,2,1,0:T(8,128)(2,1)S(1)}, u32[]{:S(2)}, u32[]{:S(2)}) %all-to-all-start) | async-done | bytes 2097184 | tf_op jit(solution)/shard_map/all_to_all | solution.py:198
  33.4 0.0 collective-permute-start.4
  33.4 1.6 %collective-permute-start.10 = (bf16[8,2,32,256]{3,2,1,0:T(8,128)(2,1)S(1)}, bf16[8,2,32,256]{3,2,1,0:T(8,128)(2,1)S(1)}, u32[]{:S(2)}, u32[]{:S(2)}) collective-permute-start(bf16[8,2,32,256]{3,2,1,0:T(8,128)(2,1)S(1)} %get-tuple-element.10.refs_2_), channel_id=1, source_target_pairs={{0,64},{8,72},{16,80},{24,88},{32,96},{40,104},{48,112},{56,120},{... | collective-permute-start | bytes 786440 | tf_op jit(solution)/shard_map/ppermute | solution.py:202
  35.0 0.9 %collective-permute-start.9 = (bf16[8,2,32,256]{3,2,1,0:T(8,128)(2,1)S(1)}, bf16[8,2,32,256]{3,2,1,0:T(8,128)(2,1)S(1)}, u32[]{:S(2)}, u32[]{:S(2)}) collective-permute-start(bf16[8,2,32,256]{3,2,1,0:T(8,128)(2,1)S(1)} %get-tuple-element.10.refs_2_), channel_id=1, source_target_pairs={{0,128},{8,136},{16,144},{24,152},{32,160},{40,168},{48,176},{56,1... | collective-permute-start | bytes 786440 | tf_op jit(solution)/shard_map/ppermute | solution.py:202
  35.9 2.4 %collective-permute-start.8 = (bf16[8,2,32,256]{3,2,1,0:T(8,128)(2,1)S(1)}, bf16[8,2,32,256]{3,2,1,0:T(8,128)(2,1)S(1)}, u32[]{:S(2)}, u32[]{:S(2)}) collective-permute-start(bf16[8,2,32,256]{3,2,1,0:T(8,128)(2,1)S(1)} %get-tuple-element.10.refs_2_), channel_id=1, source_target_pairs={{0,192},{8,200},{16,208},{24,216},{32,224},{40,232},{48,240},{56,2... | collective-permute-start | bytes 786440 | tf_op jit(solution)/shard_map/ppermute | solution.py:202
  38.3 1.0 %constant_dynamic-slice_fusion.rows_ref = bf16[128,1024]{1,0:T(8,128)(2,1)S(1)} fusion(bf16[1024,1024]{1,0:T(8,128)(2,1)} %fock_ref.1, s32[]{:T(128)S(6)} %select_n.43), kind=kLoop, calls=%fused_computation.22 | loop fusion | bytes 524292 | tf_op jit(solution)/shard_map/dynamic_slice | solution.py:215
  39.3 0.0 copy-start
  39.3 0.0 copy-start.1
  39.3 0.1 collective-permute-start.7
  39.4 7.4 %collective-permute-done.10.refs_5_ = bf16[8,2,32,256]{3,2,1,0:T(8,128)(2,1)S(1)} collective-permute-done((bf16[8,2,32,256]{3,2,1,0:T(8,128)(2,1)S(1)}, bf16[8,2,32,256]{3,2,1,0:T(8,128)(2,1)S(1)}, u32[]{:S(2)}, u32[]{:S(2)}) %collective-permute-start.10) | collective-permute-done | bytes 262176 | tf_op jit(solution)/shard_map/ppermute | solution.py:202
  46.8 5.0 %collective-permute-start.5 = (bf16[8,2,32,256]{3,2,1,0:T(8,128)(2,1)S(1)}, bf16[8,2,32,256]{3,2,1,0:T(8,128)(2,1)S(1)}, u32[]{:S(2)}, u32[]{:S(2)}) collective-permute-start(bf16[8,2,32,256]{3,2,1,0:T(8,128)(2,1)S(1)} %get-tuple-element.9.refs_2_), channel_id=1, source_target_pairs={{0,192},{8,200},{16,208},{24,216},{32,224},{40,232},{48,240},{56,2... | collective-permute-start | bytes 786440 | tf_op jit(solution)/shard_map/ppermute | solution.py:202
  51.8 0.0 collective-permute-done.8.refs_3_
  51.8 3.0 %shard_map.49 = bf16[2,1024,128]{2,1,0:T(8,128)(2,1)S(1)} custom-call(s32[4]{0:T(128)S(1)} %pad_add_fusion.at_ref, bf16[4,2,1024,128]{3,2,1,0:T(8,128)(2,1)S(1)} %all-to-all-done.refs_1_.refs_0_, bf16[4,2,1024,128]{3,2,1,0:T(8,128)(2,1)} %collective-permute-done.4.refs_2_.refs_1_, bf16[8,2,32,256]{3,2,1,0:T(8,128)(2,1)S(1)} %get-tuple-element.10.refs_2_, ...), custom_call_target="tpu_custom_call" | custom-call | flops 8589934592 | bytes 6291456 | tf_op jit(solution)/shard_map/pallas_call | solution.py:107
  54.7 2.0 %collective-permute-start.11 = (bf16[2,1024,128]{2,1,0:T(8,128)(2,1)S(1)}, bf16[2,1024,128]{2,1,0:T(8,128)(2,1)S(1)}, u32[]{:S(2)}, u32[]{:S(2)}) collective-permute-start(bf16[2,1024,128]{2,1,0:T(8,128)(2,1)S(1)} %shard_map.49), channel_id=1, source_target_pairs={{0,8},{8,0},{16,24},{24,16},{32,40},{40,32},{48,56},{56,48},{64,72... | collective-permute-start | bytes 1572872 | tf_op jit(solution)/shard_map/ppermute | solution.py:218
  56.7 4.0 %shard_map.47.fock_ref = f32[2,1024,128]{2,1,0:T(8,128)S(1)} custom-call(s32[4]{0:T(128)S(1)} %pad_add_fusion.at_ref, bf16[1024,1024]{1,0:T(8,128)(2,1)S(1)} %copy-done, bf16[128,1024]{1,0:T(8,128)(2,1)S(1)} %constant_dynamic-slice_fusion.rows_ref, bf16[2,1024,128]{2,1,0:T(8,128)(2,1)S(1)} %copy-done.1, ...), custom_call_target="tpu_custom_call" | custom-call | flops 1073741824 | bytes 4194304 | tf_op jit(solution)/shard_map/pallas_call | solution.py:64
  60.8 0.3 collective-permute-done.5.refs_3_
  61.1 3.0 %shard_map.48.mine_ref = f32[2,1024,128]{2,1,0:T(8,128)S(1)} custom-call(s32[4]{0:T(128)S(1)} %pad_add_fusion.at_ref, bf16[4,2,1024,128]{3,2,1,0:T(8,128)(2,1)S(1)} %all-to-all-done.refs_1_.refs_0_, bf16[4,2,1024,128]{3,2,1,0:T(8,128)(2,1)} %collective-permute-done.4.refs_2_.refs_1_, bf16[8,2,32,256]{3,2,1,0:T(8,128)(2,1)S(1)} %get-tuple-element.9.refs_2_, ...), custom_call_target="tpu_custom_call" | custom-call | flops 8589934592 | bytes 6291456 | tf_op jit(solution)/shard_map/pallas_call | solution.py:107
  64.0 3.2 %collective-permute-done.11.sent_ref = bf16[2,1024,128]{2,1,0:T(8,128)(2,1)S(1)} collective-permute-done((bf16[2,1024,128]{2,1,0:T(8,128)(2,1)S(1)}, bf16[2,1024,128]{2,1,0:T(8,128)(2,1)S(1)}, u32[]{:S(2)}, u32[]{:S(2)}) %collective-permute-start.11) | collective-permute-done | bytes 524320 | tf_op jit(solution)/shard_map/ppermute | solution.py:218
  67.2 0.9 %shard_map.50 = bf16[2,1024,128]{2,1,0:T(8,128)(2,1)} custom-call(f32[2,1024,128]{2,1,0:T(8,128)S(1)} %shard_map.47.fock_ref, f32[2,1024,128]{2,1,0:T(8,128)S(1)} %shard_map.48.mine_ref, bf16[2,1024,128]{2,1,0:T(8,128)(2,1)S(1)} %collective-permute-done.11.sent_ref), custom_call_target="tpu_custom_call" | custom-call | tf_op jit(solution)/shard_map/pallas_call | solution.py:136
  (18 shorter events, 0.1 us)
Async XLA Ops:
  2.6 4.5 %copy-start.2 = (bf16[4,32,4,128]{3,2,1,0:T(4,128)(2,1)S(1)}, bf16[4,32,4,128]{3,2,1,0:T(4,128)(2,1)}, u32[]{:S(2)}) copy-start(bf16[4,32,4,128]{3,2,1,0:T(4,128)(2,1)} %ints_ref.1) | copy-start | bytes 393220
  2.6 4.5 %copy-start.3 = (s32[16,16]{1,0:T(8,128)S(1)}, s32[16,16]{1,0:T(8,128)}, u32[]{:S(2)}) copy-start(s32[16,16]{1,0:T(8,128)} %mask_ref.1) | copy-start | bytes 3076
  2.6 30.8 %all-to-all-start = ((bf16[4,2,1024,128]{3,2,1,0:T(8,128)(2,1)}), bf16[4,2,1024,128]{3,2,1,0:T(8,128)(2,1)S(1)}, u32[]{:S(2)}, u32[]{:S(2)}) async-start(bf16[4,2,1024,128]{3,2,1,0:T(8,128)(2,1)} %broadcast_in_dim.2), calls=%async_computation | async-start | bytes 4194304 | tf_op jit(solution)/shard_map/all_to_all | solution.py:198
  8.1 4.4 %collective-permute-start = (bf16[2,2,32,256]{3,2,1,0:T(8,128)(2,1)S(1)}, bf16[2,2,32,256]{3,2,1,0:T(8,128)(2,1)S(1)}, u32[]{:S(2)}, u32[]{:S(2)}) collective-permute-start(bf16[2,2,32,256]{3,2,1,0:T(8,128)(2,1)S(1)} %slice_bitcast_fusion.6), channel_id=1, source_target_pairs={{0,8},{8,0},{16,24},{24,16},{32,40},{40,32},{48,56},{56,48},{64,72... | collective-permute-start | bytes 196616 | tf_op jit(solution)/shard_map/ppermute | solution.py:185
  12.5 13.0 %collective-permute-start.2 = (bf16[2,2,2,32,256]{4,3,2,1,0:T(8,128)(2,1)S(1)}, bf16[2,2,2,32,256]{4,3,2,1,0:T(8,128)(2,1)S(1)}, u32[]{:S(2)}, u32[]{:S(2)}) collective-permute-start(bf16[2,2,2,32,256]{4,3,2,1,0:T(8,128)(2,1)S(1)} %pad_maximum_fusion.2), channel_id=1, source_target_pairs={{0,32},{8,40},{16,48},{24,56},{32,0},{40,8},{48,16},{56,24},{64,96... | collective-permute-start | bytes 393224 | tf_op jit(solution)/shard_map/ppermute | solution.py:192
  19.7 11.3 %collective-permute-start.1 = (bf16[2,2,2,32,256]{4,3,2,1,0:T(8,128)(2,1)S(1)}, bf16[2,2,2,32,256]{4,3,2,1,0:T(8,128)(2,1)S(1)}, u32[]{:S(2)}, u32[]{:S(2)}) collective-permute-start(bf16[2,2,2,32,256]{4,3,2,1,0:T(8,128)(2,1)S(1)} %pad_maximum_fusion.2), channel_id=1, source_target_pairs={{0,48},{8,56},{16,0},{24,8},{32,16},{40,24},{48,32},{56,40},{64,11... | collective-permute-start | bytes 393224 | tf_op jit(solution)/shard_map/ppermute | solution.py:192
  19.7 11.4 %collective-permute-start.3 = (bf16[2,2,2,32,256]{4,3,2,1,0:T(8,128)(2,1)S(1)}, bf16[2,2,2,32,256]{4,3,2,1,0:T(8,128)(2,1)S(1)}, u32[]{:S(2)}, u32[]{:S(2)}) collective-permute-start(bf16[2,2,2,32,256]{4,3,2,1,0:T(8,128)(2,1)S(1)} %pad_maximum_fusion.2), channel_id=1, source_target_pairs={{0,16},{8,24},{16,32},{24,40},{32,48},{40,56},{48,0},{56,8},{64,80... | collective-permute-start | bytes 393224 | tf_op jit(solution)/shard_map/ppermute | solution.py:192
  33.4 18.4 %collective-permute-start.4 = (bf16[4,2,1024,128]{3,2,1,0:T(8,128)(2,1)S(1)}, bf16[4,2,1024,128]{3,2,1,0:T(8,128)(2,1)}, u32[]{:S(2)}, u32[]{:S(2)}) collective-permute-start(bf16[4,2,1024,128]{3,2,1,0:T(8,128)(2,1)S(1)} %all-to-all-done.refs_1_.refs_0_), channel_id=1, source_target_pairs={{0,1},{1,0},{2,3},{3,2},{4,5},{5,4},{6,7},{7,6},{8,9},{9,8},{10,11... | collective-permute-start | bytes 6291464 | tf_op jit(solution)/shard_map/ppermute | solution.py:181
  33.4 13.4 %collective-permute-start.10 = (bf16[8,2,32,256]{3,2,1,0:T(8,128)(2,1)S(1)}, bf16[8,2,32,256]{3,2,1,0:T(8,128)(2,1)S(1)}, u32[]{:S(2)}, u32[]{:S(2)}) collective-permute-start(bf16[8,2,32,256]{3,2,1,0:T(8,128)(2,1)S(1)} %get-tuple-element.10.refs_2_), channel_id=1, source_target_pairs={{0,64},{8,72},{16,80},{24,88},{32,96},{40,104},{48,112},{56,120},{... | collective-permute-start | bytes 786440 | tf_op jit(solution)/shard_map/ppermute | solution.py:202
  35.0 11.8 %collective-permute-start.9 = (bf16[8,2,32,256]{3,2,1,0:T(8,128)(2,1)S(1)}, bf16[8,2,32,256]{3,2,1,0:T(8,128)(2,1)S(1)}, u32[]{:S(2)}, u32[]{:S(2)}) collective-permute-start(bf16[8,2,32,256]{3,2,1,0:T(8,128)(2,1)S(1)} %get-tuple-element.10.refs_2_), channel_id=1, source_target_pairs={{0,128},{8,136},{16,144},{24,152},{32,160},{40,168},{48,176},{56,1... | collective-permute-start | bytes 786440 | tf_op jit(solution)/shard_map/ppermute | solution.py:202
  35.9 15.9 %collective-permute-start.8 = (bf16[8,2,32,256]{3,2,1,0:T(8,128)(2,1)S(1)}, bf16[8,2,32,256]{3,2,1,0:T(8,128)(2,1)S(1)}, u32[]{:S(2)}, u32[]{:S(2)}) collective-permute-start(bf16[8,2,32,256]{3,2,1,0:T(8,128)(2,1)S(1)} %get-tuple-element.10.refs_2_), channel_id=1, source_target_pairs={{0,192},{8,200},{16,208},{24,216},{32,224},{40,232},{48,240},{56,2... | collective-permute-start | bytes 786440 | tf_op jit(solution)/shard_map/ppermute | solution.py:202
  39.3 17.4 %copy-start = (bf16[1024,1024]{1,0:T(8,128)(2,1)S(1)}, bf16[1024,1024]{1,0:T(8,128)(2,1)}, u32[]{:S(2)}) copy-start(bf16[1024,1024]{1,0:T(8,128)(2,1)} %fock_ref.1) | copy-start | bytes 6291460
  39.3 17.4 %copy-start.1 = (bf16[2,1024,128]{2,1,0:T(8,128)(2,1)S(1)}, bf16[2,1024,128]{2,1,0:T(8,128)(2,1)}, u32[]{:S(2)}) copy-start(bf16[2,1024,128]{2,1,0:T(8,128)(2,1)} %refs_0_.1) | copy-start | bytes 1572868
  39.3 21.4 %collective-permute-start.7 = (bf16[8,2,32,256]{3,2,1,0:T(8,128)(2,1)S(1)}, bf16[8,2,32,256]{3,2,1,0:T(8,128)(2,1)S(1)}, u32[]{:S(2)}, u32[]{:S(2)}) collective-permute-start(bf16[8,2,32,256]{3,2,1,0:T(8,128)(2,1)S(1)} %get-tuple-element.9.refs_2_), channel_id=1, source_target_pairs={{0,64},{8,72},{16,80},{24,88},{32,96},{40,104},{48,112},{56,120},{... | collective-permute-start | bytes 786440 | tf_op jit(solution)/shard_map/ppermute | solution.py:202
  46.8 14.0 %collective-permute-start.6 = (bf16[8,2,32,256]{3,2,1,0:T(8,128)(2,1)S(1)}, bf16[8,2,32,256]{3,2,1,0:T(8,128)(2,1)S(1)}, u32[]{:S(2)}, u32[]{:S(2)}) collective-permute-start(bf16[8,2,32,256]{3,2,1,0:T(8,128)(2,1)S(1)} %get-tuple-element.9.refs_2_), channel_id=1, source_target_pairs={{0,128},{8,136},{16,144},{24,152},{32,160},{40,168},{48,176},{56,1... | collective-permute-start | bytes 786440 | tf_op jit(solution)/shard_map/ppermute | solution.py:202
  46.8 14.3 %collective-permute-start.5 = (bf16[8,2,32,256]{3,2,1,0:T(8,128)(2,1)S(1)}, bf16[8,2,32,256]{3,2,1,0:T(8,128)(2,1)S(1)}, u32[]{:S(2)}, u32[]{:S(2)}) collective-permute-start(bf16[8,2,32,256]{3,2,1,0:T(8,128)(2,1)S(1)} %get-tuple-element.9.refs_2_), channel_id=1, source_target_pairs={{0,192},{8,200},{16,208},{24,216},{32,224},{40,232},{48,240},{56,2... | collective-permute-start | bytes 786440 | tf_op jit(solution)/shard_map/ppermute | solution.py:202
  54.7 12.5 %collective-permute-start.11 = (bf16[2,1024,128]{2,1,0:T(8,128)(2,1)S(1)}, bf16[2,1024,128]{2,1,0:T(8,128)(2,1)S(1)}, u32[]{:S(2)}, u32[]{:S(2)}) collective-permute-start(bf16[2,1024,128]{2,1,0:T(8,128)(2,1)S(1)} %shard_map.49), channel_id=1, source_target_pairs={{0,8},{8,0},{16,24},{24,16},{32,40},{40,32},{48,56},{56,48},{64,72... | collective-permute-start | bytes 1572872 | tf_op jit(solution)/shard_map/ppermute | solution.py:218

commit v4 on v3

--- a/solution.py
+++ b/solution.py
@@ -21,7 +21,7 @@
 
 VM = 16
 COST = 8
-CROWS = 1024
+CROWS = 512
 CHUNKS = 4
 MINE_COST = 8
 
@@ -73,7 +73,7 @@
     )(at, fock_vv, fock_rows, *amps)
 
 
-def cycle_kernel(at_ref, *refs):
+def cycle_kernel(first, at_ref, *refs):
     held, out_ref, refs = refs[-1], refs[-2], refs[:-2]
     ints, amps = refs[-NY:], refs[:-NY]
     y, z, core = at_ref[0], at_ref[1], at_ref[3]
@@ -94,37 +94,40 @@
 
     @pl.loop(0, out_ref.shape[1] // CROWS)
     def _(r):
-        at = pl.ds(pl.multiple_of(r * CROWS, CROWS), CROWS)
+        to = pl.ds(pl.multiple_of(r * CROWS, CROWS), CROWS)
+        at = pl.ds(pl.multiple_of(first + r * CROWS, CROWS), CROWS)
         lhs = jnp.concatenate([a[p, at, :] for p in range(pairs) for a in amps], axis=1)
         total = jnp.dot(lhs, rhs, preferred_element_type=jnp.float32)
         for p in range(pairs):
-            out_ref[p, at, :] = total[:, p * width : (p + 1) * width].astype(out_ref.dtype)
-
-
-def cycle_sum(at, amps, ints, dtype, cost):
+            out_ref[p, to, :] = total[:, p * width : (p + 1) * width].astype(out_ref.dtype)
+
+
+def cycle_sum(at, amps, ints, dtype, cost, first, rows):
     n_z, pairs, depth, cols = ints[0].shape
-    shape = amps[0].shape[1:]
-    return pl.pallas_call(
-        cycle_kernel,
+    shape = (pairs, rows, amps[0].shape[-1])
+    return pl.pallas_call(
+        functools.partial(cycle_kernel, first),
         out_shape=jax.ShapeDtypeStruct(shape, dtype),
         in_specs=[SMEM] + [VMEM] * (len(amps) + len(ints)),
         out_specs=VMEM,
         scratch_shapes=[pltpu.VMEM((NY, 2, pairs, 2, 2 * depth, cols), jnp.bfloat16)],
         compiler_params=pltpu.CompilerParams(vmem_limit_bytes=VM * MIB),
         cost_estimate=pl.CostEstimate(
-            flops=cost * shape[0] * shape[1] * shape[1] * shape[2] * 4,
+            flops=cost * pairs * rows * 8 * rows * cols,
             bytes_accessed=6 * MIB,
             transcendentals=0,
         ),
     )(at, *amps, *ints)
 
 
-def add_kernel(fock_ref, mine_ref, sent_ref, out_ref, done, sems):
+def add_kernel(fock_ref, mine_ref, low_ref, high_ref, out_ref, done, sems):
     rows = out_ref.shape[1] // CHUNKS
     copies = []
     for i in range(CHUNKS):
         at = pl.ds(i * rows, rows)
-        cycle = (mine_ref[:, at, :] + sent_ref[:, at, :].astype(jnp.float32)).astype(jnp.bfloat16)
+        sent_ref, part = (low_ref, i) if i < CHUNKS // 2 else (high_ref, i - CHUNKS // 2)
+        sent = sent_ref[:, pl.ds(part * rows, rows), :].astype(jnp.float32)
+        cycle = (mine_ref[:, at, :] + sent).astype(jnp.bfloat16)
         done[:, at, :] = (fock_ref[:, at, :] + cycle.astype(jnp.float32)).astype(jnp.bfloat16)
         copies.append(pltpu.make_async_copy(done.at[:, at, :], out_ref.at[:, at, :], sems.at[i]))
         copies[-1].start()
@@ -132,15 +135,15 @@
         copy.wait()
 
 
-def add(fock_part, mine, sent):
+def add(fock_part, mine, low, high):
     return pl.pallas_call(
         add_kernel,
-        out_shape=jax.ShapeDtypeStruct(sent.shape, jnp.bfloat16),
-        in_specs=[VMEM] * 3,
+        out_shape=jax.ShapeDtypeStruct(mine.shape, jnp.bfloat16),
+        in_specs=[VMEM] * 4,
         out_specs=pl.BlockSpec(memory_space=pl.ANY),
-        scratch_shapes=[pltpu.VMEM(sent.shape, jnp.bfloat16), pltpu.SemaphoreType.DMA((CHUNKS,))],
+        scratch_shapes=[pltpu.VMEM(mine.shape, jnp.bfloat16), pltpu.SemaphoreType.DMA((CHUNKS,))],
         compiler_params=pltpu.CompilerParams(vmem_limit_bytes=VM * MIB),
-    )(fock_part, mine, sent)
+    )(fock_part, mine, low, high)
 
 
 def prepare_kernel(at_ref, mask_ref, ints_ref, out_ref):
@@ -209,14 +212,21 @@
     rows = along_z(pair_along_z(halves, at[1]))
     gathered = spread(amplitudes, "ints", X_GROUPS)
     gathered, *rows = lax.optimization_barrier((gathered, *rows))
-    partners, mine = along_y(rows[0]), along_y(rows[1])
+    partners = along_y(rows[0])
+    second, _ = lax.optimization_barrier((rows[1], partners[2]))
+    mine = along_y(second)
     own = [gathered, swap(gathered)]
 
     fock_rows = lax.dynamic_slice_in_dim(fock_vv, ints * amplitudes.shape[2], amplitudes.shape[2], 0)
     fock_part = fock_terms(at, fock_vv, fock_rows, [amplitudes, *own])
-    sent = cycle_sum(at, own, partners, jnp.bfloat16, COST)
-    sent = lax.ppermute(sent, "amp", Z_PAIR)
-    return add(fock_part, cycle_sum(at, own, mine, jnp.float32, MINE_COST), sent)
+    rows = amplitudes.shape[1]
+    sent = []
+    for first in range(0, rows, rows // 2):
+        half = cycle_sum(at, own, partners, jnp.bfloat16, COST, first, rows // 2)
+        sent.append(lax.ppermute(half, "amp", Z_PAIR))
+    mine[0], _ = lax.optimization_barrier((mine[0], fock_part))
+    mine = cycle_sum(at, own, mine, jnp.float32, MINE_COST, 0, rows)
+    return add(fock_part, mine, *sent)
 
 
 def solution(mesh):

time: 68.4 us -> 67.3 us (0.984)
  starting transfers between devices: 28.6 us -> 25.8 us
  Pallas kernels: 11.7 us -> 13.8 us
    ppermute x6, starting transfers between devices: 9.99 us -> 6.84 us  [along_y(): return [row] + [lax.ppermute(row, 'amp', Y_RING(-e)) for e in (1, 2, 3)]]
    pallas_call x3 -> x4, Pallas kernels: 6.77 us -> 8.89 us  [the longest x3 8.03 us: cycle_sum(): pl.pallas_call(functools.partial(cycle_kernel, first), out_shape=jax.Shap...]
    ppermute x1 -> x2, waiting for transfers between devices: 3.17 us -> 1.84 us  [body(): sent.append(lax.ppermute(half, 'amp', Z_PAIR))]
    ppermute x6, waiting for transfers between devices: 7.66 us -> 8.58 us  [along_y(): return [row] + [lax.ppermute(row, 'amp', Y_RING(-e)) for e in (1, 2, 3)]]
    ppermute x1 -> x2, starting transfers between devices: 2 us -> 2.34 us  [body(): sent.append(lax.ppermute(half, 'amp', Z_PAIR))]
  transfers between devices with their start and end apart: 13 -> 14, of which waited for: 7 -> 7; matrix products, arithmetic and copies ran while one was open for 2% -> 2% of each run, Pallas kernels for 16% -> 19%
where the time goes in v4:
time: 67.3 us; the launch traced here: 67 us
  starting transfers between devices  25.8 us (38%)
  waiting for transfers between devices  23.4 us (35%)
  Pallas kernels  13.8 us (21%)
  local copies, waits for them, and re-layouts  3.67 us (5%)
    ppermute x3, starting transfers between devices, along_z(): lax.ppermute(pair, 'amp', Z_RING(-2 * g))  10.2 us
    ppermute x6, waiting for transfers between devices, along_y(): return [row] + [lax.ppermute(row, 'amp', Y_RING(-e)) for e in (1, 2, 3)]  8.58 us
    ppermute x3, waiting for transfers between devices, along_z(): lax.ppermute(pair, 'amp', Z_RING(-2 * g))  8.39 us
    pallas_call x3, Pallas kernels, cycle_sum(): pl.pallas_call(functools.partial(cycle_kernel, first), out_shape=jax.Shap...  8.03 us
    ppermute x6, starting transfers between devices, along_y(): return [row] + [lax.ppermute(row, 'amp', Y_RING(-e)) for e in (1, 2, 3)]  6.84 us
    all_to_all x1, starting transfers between devices, spread(): return lax.all_to_all(a, axis, 0, 0, axis_index_groups=groups)  4.42 us
    pallas_call x1, Pallas kernels, fock_terms(): pl.pallas_call(fock_kernel, out_shape=jax.ShapeDtypeStruct((pairs, width,...  4 us
    broadcast_in_dim x1, local copies, waits for them, and re-layouts, spread(): a = jnp.broadcast_to(a[None], (len(groups[0]),) + a.shape)  2.65 us
  transfers between devices with their start and end apart: 14, of which 7 were waited for; matrix products, arithmetic and copies ran while one was open for 2% of the time, Pallas kernels for 19%

profile of v4, /device:TPU:8, one launch (start us, length us, event | category | flops | bytes accessed | tf_op | source)
XLA Modules:
  0.0 67.0 jit_solution(13845039914220214944)
XLA Ops:
  0.0 2.6 %broadcast_in_dim.2 = bf16[4,2,1024,128]{3,2,1,0:T(8,128)(2,1)} broadcast(bf16[2,1024,128]{2,1,0:T(8,128)(2,1)} %refs_0_.1), dimensions={1,2,3} | broadcast | bytes 2621440 | tf_op jit(solution)/shard_map/broadcast_in_dim | solution.py:200
  2.7 4.4 %all-to-all-start = ((bf16[4,2,1024,128]{3,2,1,0:T(8,128)(2,1)}), bf16[4,2,1024,128]{3,2,1,0:T(8,128)(2,1)S(1)}, u32[]{:S(2)}, u32[]{:S(2)}) async-start(bf16[4,2,1024,128]{3,2,1,0:T(8,128)(2,1)} %broadcast_in_dim.2), calls=%async_computation | async-start | bytes 4194304 | tf_op jit(solution)/shard_map/all_to_all | solution.py:201
  7.1 0.1 pad_add_fusion.at_ref
  7.2 0.9 %shard_map.46 = bf16[2,2,2,32,256]{4,3,2,1,0:T(8,128)(2,1)S(1)} custom-call(s32[4]{0:T(128)S(1)} %pad_add_fusion.at_ref, s32[16,16]{1,0:T(8,128)S(1)} %copy-done.3, bf16[4,32,4,128]{3,2,1,0:T(4,128)(2,1)S(1)} %copy-done.2), custom_call_target="tpu_custom_call" | custom-call | tf_op jit(solution)/shard_map/pallas_call | solution.py:170
  8.1 2.0 %collective-permute-start = (bf16[2,2,32,256]{3,2,1,0:T(8,128)(2,1)S(1)}, bf16[2,2,32,256]{3,2,1,0:T(8,128)(2,1)S(1)}, u32[]{:S(2)}, u32[]{:S(2)}) collective-permute-start(bf16[2,2,32,256]{3,2,1,0:T(8,128)(2,1)S(1)} %slice_bitcast_fusion.6), channel_id=1, source_target_pairs={{0,8},{8,0},{16,24},{24,16},{32,40},{40,32},{48,56},{56,48},{64,72... | collective-permute-start | bytes 196616 | tf_op jit(solution)/shard_map/ppermute | solution.py:188
  10.1 2.3 %collective-permute-done = bf16[2,2,32,256]{3,2,1,0:T(8,128)(2,1)S(1)} collective-permute-done((bf16[2,2,32,256]{3,2,1,0:T(8,128)(2,1)S(1)}, bf16[2,2,32,256]{3,2,1,0:T(8,128)(2,1)S(1)}, u32[]{:S(2)}, u32[]{:S(2)}) %collective-permute-start) | collective-permute-done | bytes 65568 | tf_op jit(solution)/shard_map/ppermute | solution.py:188
  12.5 7.3 %collective-permute-start.2 = (bf16[2,2,2,32,256]{4,3,2,1,0:T(8,128)(2,1)S(1)}, bf16[2,2,2,32,256]{4,3,2,1,0:T(8,128)(2,1)S(1)}, u32[]{:S(2)}, u32[]{:S(2)}) collective-permute-start(bf16[2,2,2,32,256]{4,3,2,1,0:T(8,128)(2,1)S(1)} %pad_maximum_fusion.2), channel_id=1, source_target_pairs={{0,32},{8,40},{16,48},{24,56},{32,0},{40,8},{48,16},{56,24},{64,96... | collective-permute-start | bytes 393224 | tf_op jit(solution)/shard_map/ppermute | solution.py:195
  19.7 0.0 collective-permute-start.1
  19.7 2.9 %collective-permute-start.3 = (bf16[2,2,2,32,256]{4,3,2,1,0:T(8,128)(2,1)S(1)}, bf16[2,2,2,32,256]{4,3,2,1,0:T(8,128)(2,1)S(1)}, u32[]{:S(2)}, u32[]{:S(2)}) collective-permute-start(bf16[2,2,2,32,256]{4,3,2,1,0:T(8,128)(2,1)S(1)} %pad_maximum_fusion.2), channel_id=1, source_target_pairs={{0,16},{8,24},{16,32},{24,40},{32,48},{40,56},{48,0},{56,8},{64,80... | collective-permute-start | bytes 393224 | tf_op jit(solution)/shard_map/ppermute | solution.py:195
  22.7 2.8 %collective-permute-done.2 = bf16[2,2,2,32,256]{4,3,2,1,0:T(8,128)(2,1)S(1)} collective-permute-done((bf16[2,2,2,32,256]{4,3,2,1,0:T(8,128)(2,1)S(1)}, bf16[2,2,2,32,256]{4,3,2,1,0:T(8,128)(2,1)S(1)}, u32[]{:S(2)}, u32[]{:S(2)}) %collective-permute-start.2) | collective-permute-done | bytes 131104 | tf_op jit(solution)/shard_map/ppermute | solution.py:195
  25.5 5.6 %collective-permute-done.1 = bf16[2,2,2,32,256]{4,3,2,1,0:T(8,128)(2,1)S(1)} collective-permute-done((bf16[2,2,2,32,256]{4,3,2,1,0:T(8,128)(2,1)S(1)}, bf16[2,2,2,32,256]{4,3,2,1,0:T(8,128)(2,1)S(1)}, u32[]{:S(2)}, u32[]{:S(2)}) %collective-permute-start.1) | collective-permute-done | bytes 131104 | tf_op jit(solution)/shard_map/ppermute | solution.py:195
  31.1 0.0 collective-permute-done.3
  31.1 0.1 pad_maximum_fusion
  31.2 2.2 %all-to-all-done.refs_1_.refs_0_ = bf16[4,2,1024,128]{3,2,1,0:T(8,128)(2,1)S(1)} async-done(((bf16[4,2,1024,128]{3,2,1,0:T(8,128)(2,1)}), bf16[4,2,1024,128]{3,2,1,0:T(8,128)(2,1)S(1)}, u32[]{:S(2)}, u32[]{:S(2)}) %all-to-all-start) | async-done | bytes 2097184 | tf_op jit(solution)/shard_map/all_to_all | solution.py:201
  33.4 0.0 collective-permute-start.4
  33.4 2.3 %collective-permute-start.5 = (bf16[8,2,32,256]{3,2,1,0:T(8,128)(2,1)S(1)}, bf16[8,2,32,256]{3,2,1,0:T(8,128)(2,1)S(1)}, u32[]{:S(2)}, u32[]{:S(2)}) collective-permute-start(bf16[8,2,32,256]{3,2,1,0:T(8,128)(2,1)S(1)} %get-tuple-element.12.refs_2_), channel_id=1, source_target_pairs={{0,128},{8,136},{16,144},{24,152},{32,160},{40,168},{48,176},{56,1... | collective-permute-start | bytes 786440 | tf_op jit(solution)/shard_map/ppermute | solution.py:205
  35.7 2.0 %collective-permute-start.9 = (bf16[8,2,32,256]{3,2,1,0:T(8,128)(2,1)S(1)}, bf16[8,2,32,256]{3,2,1,0:T(8,128)(2,1)S(1)}, u32[]{:S(2)}, u32[]{:S(2)}) collective-permute-start(bf16[8,2,32,256]{3,2,1,0:T(8,128)(2,1)S(1)} %get-tuple-element.12.refs_2_), channel_id=1, source_target_pairs={{0,192},{8,200},{16,208},{24,216},{32,224},{40,232},{48,240},{56,2... | collective-permute-start | bytes 786440 | tf_op jit(solution)/shard_map/ppermute | solution.py:205
  37.7 1.0 %constant_dynamic-slice_fusion.rows_ref = bf16[128,1024]{1,0:T(8,128)(2,1)S(1)} fusion(bf16[1024,1024]{1,0:T(8,128)(2,1)} %fock_ref.1, s32[]{:T(128)S(6)} %select_n.43), kind=kLoop, calls=%fused_computation.22 | loop fusion | bytes 524292 | tf_op jit(solution)/shard_map/dynamic_slice | solution.py:220
  38.7 5.4 %collective-permute-done.5.refs_4_ = bf16[8,2,32,256]{3,2,1,0:T(8,128)(2,1)S(1)} collective-permute-done((bf16[8,2,32,256]{3,2,1,0:T(8,128)(2,1)S(1)}, bf16[8,2,32,256]{3,2,1,0:T(8,128)(2,1)S(1)}, u32[]{:S(2)}, u32[]{:S(2)}) %collective-permute-start.5) | collective-permute-done | bytes 262176 | tf_op jit(solution)/shard_map/ppermute | solution.py:205
  44.1 1.6 %collective-permute-start.8 = (bf16[8,2,32,256]{3,2,1,0:T(8,128)(2,1)S(1)}, bf16[8,2,32,256]{3,2,1,0:T(8,128)(2,1)S(1)}, u32[]{:S(2)}, u32[]{:S(2)}) collective-permute-start(bf16[8,2,32,256]{3,2,1,0:T(8,128)(2,1)S(1)} %get-tuple-element.14.refs_2_), channel_id=1, source_target_pairs={{0,64},{8,72},{16,80},{24,88},{32,96},{40,104},{48,112},{56,120},{... | collective-permute-start | bytes 786440 | tf_op jit(solution)/shard_map/ppermute | solution.py:205
  45.6 0.9 %collective-permute-start.7 = (bf16[8,2,32,256]{3,2,1,0:T(8,128)(2,1)S(1)}, bf16[8,2,32,256]{3,2,1,0:T(8,128)(2,1)S(1)}, u32[]{:S(2)}, u32[]{:S(2)}) collective-permute-start(bf16[8,2,32,256]{3,2,1,0:T(8,128)(2,1)S(1)} %get-tuple-element.14.refs_2_), channel_id=1, source_target_pairs={{0,128},{8,136},{16,144},{24,152},{32,160},{40,168},{48,176},{56,1... | collective-permute-start | bytes 786440 | tf_op jit(solution)/shard_map/ppermute | solution.py:205
  46.6 3.2 %collective-permute-done.10.refs_5_ = bf16[8,2,32,256]{3,2,1,0:T(8,128)(2,1)S(1)} collective-permute-done((bf16[8,2,32,256]{3,2,1,0:T(8,128)(2,1)S(1)}, bf16[8,2,32,256]{3,2,1,0:T(8,128)(2,1)S(1)}, u32[]{:S(2)}, u32[]{:S(2)}) %collective-permute-start.10) | collective-permute-done | bytes 262176 | tf_op jit(solution)/shard_map/ppermute | solution.py:205
  49.8 2.4 %shard_map.49 = bf16[2,512,128]{2,1,0:T(8,128)(2,1)S(1)} custom-call(s32[4]{0:T(128)S(1)} %pad_add_fusion.at_ref, bf16[4,2,1024,128]{3,2,1,0:T(8,128)(2,1)S(1)} %all-to-all-done.refs_1_.refs_0_, bf16[4,2,1024,128]{3,2,1,0:T(8,128)(2,1)} %collective-permute-done.4.refs_2_.refs_1_, bf16[8,2,32,256]{3,2,1,0:T(8,128)(2,1)S(1)} %get-tuple-element.12.refs_2_, ...), custom_call_target="tpu_custom_call" | custom-call | flops 8589934592 | bytes 6291456 | tf_op jit(solution)/shard_map/pallas_call | solution.py:108
  52.2 0.0 copy-start
  52.3 0.0 copy-start.1
  52.3 2.0 %collective-permute-start.11 = (bf16[2,512,128]{2,1,0:T(8,128)(2,1)S(1)}, bf16[2,512,128]{2,1,0:T(8,128)(2,1)S(1)}, u32[]{:S(2)}, u32[]{:S(2)}) collective-permute-start(bf16[2,512,128]{2,1,0:T(8,128)(2,1)S(1)} %shard_map.49), channel_id=1, source_target_pairs={{0,8},{8,0},{16,24},{24,16},{32,40},{40,32},{48,56},{56,48},{64,72... | collective-permute-start | bytes 786440 | tf_op jit(solution)/shard_map/ppermute | solution.py:226
  54.3 2.4 %shard_map.50 = bf16[2,512,128]{2,1,0:T(8,128)(2,1)S(1)} custom-call(s32[4]{0:T(128)S(1)} %pad_add_fusion.at_ref, bf16[4,2,1024,128]{3,2,1,0:T(8,128)(2,1)S(1)} %all-to-all-done.refs_1_.refs_0_, bf16[4,2,1024,128]{3,2,1,0:T(8,128)(2,1)} %collective-permute-done.4.refs_2_.refs_1_, bf16[8,2,32,256]{3,2,1,0:T(8,128)(2,1)S(1)} %get-tuple-element.12.refs_2_, ...), custom_call_target="tpu_custom_call" | custom-call | flops 8589934592 | bytes 6291456 | tf_op jit(solution)/shard_map/pallas_call | solution.py:108
  56.7 0.3 collective-permute-start.12
  57.0 4.0 %shard_map.47.fock_ref = f32[2,1024,128]{2,1,0:T(8,128)S(1)} custom-call(s32[4]{0:T(128)S(1)} %pad_add_fusion.at_ref, bf16[1024,1024]{1,0:T(8,128)(2,1)S(1)} %copy-done, bf16[128,1024]{1,0:T(8,128)(2,1)S(1)} %constant_dynamic-slice_fusion.rows_ref, bf16[2,1024,128]{2,1,0:T(8,128)(2,1)S(1)} %copy-done.1, ...), custom_call_target="tpu_custom_call" | custom-call | flops 1073741824 | bytes 4194304 | tf_op jit(solution)/shard_map/pallas_call | solution.py:64
  61.1 3.2 %shard_map.48.mine_ref = f32[2,1024,128]{2,1,0:T(8,128)S(1)} custom-call(s32[4]{0:T(128)S(1)} %pad_add_fusion.at_ref, bf16[4,2,1024,128]{3,2,1,0:T(8,128)(2,1)S(1)} %all-to-all-done.refs_1_.refs_0_, bf16[4,2,1024,128]{3,2,1,0:T(8,128)(2,1)} %collective-permute-done.4.refs_2_.refs_1_, bf16[8,2,32,256]{3,2,1,0:T(8,128)(2,1)S(1)} %get-tuple-element.14.refs_2_, ...), custom_call_target="tpu_custom_call" | custom-call | flops 34359738368 | bytes 6291456 | tf_op jit(solution)/shard_map/pallas_call | solution.py:108
  64.3 1.8 %collective-permute-done.12.high_ref = bf16[2,512,128]{2,1,0:T(8,128)(2,1)S(1)} collective-permute-done((bf16[2,512,128]{2,1,0:T(8,128)(2,1)S(1)}, bf16[2,512,128]{2,1,0:T(8,128)(2,1)S(1)}, u32[]{:S(2)}, u32[]{:S(2)}) %collective-permute-start.12) | collective-permute-done | bytes 262176 | tf_op jit(solution)/shard_map/ppermute | solution.py:226
  66.1 0.9 %shard_map.51 = bf16[2,1024,128]{2,1,0:T(8,128)(2,1)} custom-call(f32[2,1024,128]{2,1,0:T(8,128)S(1)} %shard_map.47.fock_ref, f32[2,1024,128]{2,1,0:T(8,128)S(1)} %shard_map.48.mine_ref, bf16[2,512,128]{2,1,0:T(8,128)(2,1)S(1)} %collective-permute-done.11.low_ref, bf16[2,512,128]{2,1,0:T(8,128)(2,1)S(1)} %collective-permute-done.12.high_ref), custom_call_target="tpu_custom_call" | custom-call | tf_op jit(solution)/shard_map/pallas_call | solution.py:139
  (21 shorter events, 0.1 us)
Async XLA Ops:
  2.7 4.5 %copy-start.2 = (bf16[4,32,4,128]{3,2,1,0:T(4,128)(2,1)S(1)}, bf16[4,32,4,128]{3,2,1,0:T(4,128)(2,1)}, u32[]{:S(2)}) copy-start(bf16[4,32,4,128]{3,2,1,0:T(4,128)(2,1)} %ints_ref.1) | copy-start | bytes 393220
  2.7 4.5 %copy-start.3 = (s32[16,16]{1,0:T(8,128)S(1)}, s32[16,16]{1,0:T(8,128)}, u32[]{:S(2)}) copy-start(s32[16,16]{1,0:T(8,128)} %mask_ref.1) | copy-start | bytes 3076
  2.7 30.8 %all-to-all-start = ((bf16[4,2,1024,128]{3,2,1,0:T(8,128)(2,1)}), bf16[4,2,1024,128]{3,2,1,0:T(8,128)(2,1)S(1)}, u32[]{:S(2)}, u32[]{:S(2)}) async-start(bf16[4,2,1024,128]{3,2,1,0:T(8,128)(2,1)} %broadcast_in_dim.2), calls=%async_computation | async-start | bytes 4194304 | tf_op jit(solution)/shard_map/all_to_all | solution.py:201
  8.1 4.4 %collective-permute-start = (bf16[2,2,32,256]{3,2,1,0:T(8,128)(2,1)S(1)}, bf16[2,2,32,256]{3,2,1,0:T(8,128)(2,1)S(1)}, u32[]{:S(2)}, u32[]{:S(2)}) collective-permute-start(bf16[2,2,32,256]{3,2,1,0:T(8,128)(2,1)S(1)} %slice_bitcast_fusion.6), channel_id=1, source_target_pairs={{0,8},{8,0},{16,24},{24,16},{32,40},{40,32},{48,56},{56,48},{64,72... | collective-permute-start | bytes 196616 | tf_op jit(solution)/shard_map/ppermute | solution.py:188
  12.5 13.0 %collective-permute-start.2 = (bf16[2,2,2,32,256]{4,3,2,1,0:T(8,128)(2,1)S(1)}, bf16[2,2,2,32,256]{4,3,2,1,0:T(8,128)(2,1)S(1)}, u32[]{:S(2)}, u32[]{:S(2)}) collective-permute-start(bf16[2,2,2,32,256]{4,3,2,1,0:T(8,128)(2,1)S(1)} %pad_maximum_fusion.2), channel_id=1, source_target_pairs={{0,32},{8,40},{16,48},{24,56},{32,0},{40,8},{48,16},{56,24},{64,96... | collective-permute-start | bytes 393224 | tf_op jit(solution)/shard_map/ppermute | solution.py:195
  19.7 11.3 %collective-permute-start.1 = (bf16[2,2,2,32,256]{4,3,2,1,0:T(8,128)(2,1)S(1)}, bf16[2,2,2,32,256]{4,3,2,1,0:T(8,128)(2,1)S(1)}, u32[]{:S(2)}, u32[]{:S(2)}) collective-permute-start(bf16[2,2,2,32,256]{4,3,2,1,0:T(8,128)(2,1)S(1)} %pad_maximum_fusion.2), channel_id=1, source_target_pairs={{0,48},{8,56},{16,0},{24,8},{32,16},{40,24},{48,32},{56,40},{64,11... | collective-permute-start | bytes 393224 | tf_op jit(solution)/shard_map/ppermute | solution.py:195
  19.7 11.4 %collective-permute-start.3 = (bf16[2,2,2,32,256]{4,3,2,1,0:T(8,128)(2,1)S(1)}, bf16[2,2,2,32,256]{4,3,2,1,0:T(8,128)(2,1)S(1)}, u32[]{:S(2)}, u32[]{:S(2)}) collective-permute-start(bf16[2,2,2,32,256]{4,3,2,1,0:T(8,128)(2,1)S(1)} %pad_maximum_fusion.2), channel_id=1, source_target_pairs={{0,16},{8,24},{16,32},{24,40},{32,48},{40,56},{48,0},{56,8},{64,80... | collective-permute-start | bytes 393224 | tf_op jit(solution)/shard_map/ppermute | solution.py:195
  33.4 16.4 %collective-permute-start.4 = (bf16[4,2,1024,128]{3,2,1,0:T(8,128)(2,1)S(1)}, bf16[4,2,1024,128]{3,2,1,0:T(8,128)(2,1)}, u32[]{:S(2)}, u32[]{:S(2)}) collective-permute-start(bf16[4,2,1024,128]{3,2,1,0:T(8,128)(2,1)S(1)} %all-to-all-done.refs_1_.refs_0_), channel_id=1, source_target_pairs={{0,1},{1,0},{2,3},{3,2},{4,5},{5,4},{6,7},{7,6},{8,9},{9,8},{10,11... | collective-permute-start | bytes 6291464 | tf_op jit(solution)/shard_map/ppermute | solution.py:184
  33.4 10.7 %collective-permute-start.5 = (bf16[8,2,32,256]{3,2,1,0:T(8,128)(2,1)S(1)}, bf16[8,2,32,256]{3,2,1,0:T(8,128)(2,1)S(1)}, u32[]{:S(2)}, u32[]{:S(2)}) collective-permute-start(bf16[8,2,32,256]{3,2,1,0:T(8,128)(2,1)S(1)} %get-tuple-element.12.refs_2_), channel_id=1, source_target_pairs={{0,128},{8,136},{16,144},{24,152},{32,160},{40,168},{48,176},{56,1... | collective-permute-start | bytes 786440 | tf_op jit(solution)/shard_map/ppermute | solution.py:205
  35.7 14.1 %collective-permute-start.10 = (bf16[8,2,32,256]{3,2,1,0:T(8,128)(2,1)S(1)}, bf16[8,2,32,256]{3,2,1,0:T(8,128)(2,1)S(1)}, u32[]{:S(2)}, u32[]{:S(2)}) collective-permute-start(bf16[8,2,32,256]{3,2,1,0:T(8,128)(2,1)S(1)} %get-tuple-element.12.refs_2_), channel_id=1, source_target_pairs={{0,64},{8,72},{16,80},{24,88},{32,96},{40,104},{48,112},{56,120},{... | collective-permute-start | bytes 786440 | tf_op jit(solution)/shard_map/ppermute | solution.py:205
  35.7 14.1 %collective-permute-start.9 = (bf16[8,2,32,256]{3,2,1,0:T(8,128)(2,1)S(1)}, bf16[8,2,32,256]{3,2,1,0:T(8,128)(2,1)S(1)}, u32[]{:S(2)}, u32[]{:S(2)}) collective-permute-start(bf16[8,2,32,256]{3,2,1,0:T(8,128)(2,1)S(1)} %get-tuple-element.12.refs_2_), channel_id=1, source_target_pairs={{0,192},{8,200},{16,208},{24,216},{32,224},{40,232},{48,240},{56,2... | collective-permute-start | bytes 786440 | tf_op jit(solution)/shard_map/ppermute | solution.py:205
  44.1 17.0 %collective-permute-start.8 = (bf16[8,2,32,256]{3,2,1,0:T(8,128)(2,1)S(1)}, bf16[8,2,32,256]{3,2,1,0:T(8,128)(2,1)S(1)}, u32[]{:S(2)}, u32[]{:S(2)}) collective-permute-start(bf16[8,2,32,256]{3,2,1,0:T(8,128)(2,1)S(1)} %get-tuple-element.14.refs_2_), channel_id=1, source_target_pairs={{0,64},{8,72},{16,80},{24,88},{32,96},{40,104},{48,112},{56,120},{... | collective-permute-start | bytes 786440 | tf_op jit(solution)/shard_map/ppermute | solution.py:205
  45.6 15.4 %collective-permute-start.7 = (bf16[8,2,32,256]{3,2,1,0:T(8,128)(2,1)S(1)}, bf16[8,2,32,256]{3,2,1,0:T(8,128)(2,1)S(1)}, u32[]{:S(2)}, u32[]{:S(2)}) collective-permute-start(bf16[8,2,32,256]{3,2,1,0:T(8,128)(2,1)S(1)} %get-tuple-element.14.refs_2_), channel_id=1, source_target_pairs={{0,128},{8,136},{16,144},{24,152},{32,160},{40,168},{48,176},{56,1... | collective-permute-start | bytes 786440 | tf_op jit(solution)/shard_map/ppermute | solution.py:205
  49.8 11.3 %collective-permute-start.6 = (bf16[8,2,32,256]{3,2,1,0:T(8,128)(2,1)S(1)}, bf16[8,2,32,256]{3,2,1,0:T(8,128)(2,1)S(1)}, u32[]{:S(2)}, u32[]{:S(2)}) collective-permute-start(bf16[8,2,32,256]{3,2,1,0:T(8,128)(2,1)S(1)} %get-tuple-element.14.refs_2_), channel_id=1, source_target_pairs={{0,192},{8,200},{16,208},{24,216},{32,224},{40,232},{48,240},{56,2... | collective-permute-start | bytes 786440 | tf_op jit(solution)/shard_map/ppermute | solution.py:205
  52.2 4.8 %copy-start = (bf16[1024,1024]{1,0:T(8,128)(2,1)S(1)}, bf16[1024,1024]{1,0:T(8,128)(2,1)}, u32[]{:S(2)}) copy-start(bf16[1024,1024]{1,0:T(8,128)(2,1)} %fock_ref.1) | copy-start | bytes 6291460
  52.3 4.8 %copy-start.1 = (bf16[2,1024,128]{2,1,0:T(8,128)(2,1)S(1)}, bf16[2,1024,128]{2,1,0:T(8,128)(2,1)}, u32[]{:S(2)}) copy-start(bf16[2,1024,128]{2,1,0:T(8,128)(2,1)} %refs_0_.1) | copy-start | bytes 1572868
  52.3 12.0 %collective-permute-start.11 = (bf16[2,512,128]{2,1,0:T(8,128)(2,1)S(1)}, bf16[2,512,128]{2,1,0:T(8,128)(2,1)S(1)}, u32[]{:S(2)}, u32[]{:S(2)}) collective-permute-start(bf16[2,512,128]{2,1,0:T(8,128)(2,1)S(1)} %shard_map.49), channel_id=1, source_target_pairs={{0,8},{8,0},{16,24},{24,16},{32,40},{40,32},{48,56},{56,48},{64,72... | collective-permute-start | bytes 786440 | tf_op jit(solution)/shard_map/ppermute | solution.py:226
  56.7 9.4 %collective-permute-start.12 = (bf16[2,512,128]{2,1,0:T(8,128)(2,1)S(1)}, bf16[2,512,128]{2,1,0:T(8,128)(2,1)S(1)}, u32[]{:S(2)}, u32[]{:S(2)}) collective-permute-start(bf16[2,512,128]{2,1,0:T(8,128)(2,1)S(1)} %shard_map.50), channel_id=1, source_target_pairs={{0,8},{8,0},{16,24},{24,16},{32,40},{40,32},{48,56},{56,48},{64,72... | collective-permute-start | bytes 786440 | tf_op jit(solution)/shard_map/ppermute | solution.py:226

commit v5 on v4

--- a/solution.py
+++ b/solution.py
@@ -208,7 +208,9 @@
 def body(amplitudes, fock_vv, cycle_ints, tile_mask):
     amp, ints = lax.axis_index("amp"), lax.axis_index("ints")
     at = jnp.stack([amp // NZ, amp % NZ, ints // 2, ints % 2]).astype(jnp.int32)
+    fock_rows = lax.dynamic_slice_in_dim(fock_vv, ints * amplitudes.shape[2], amplitudes.shape[2], 0)
     halves = prepare(at, tile_mask, cycle_ints)
+    halves, fock_rows = lax.optimization_barrier((halves, fock_rows))
     rows = along_z(pair_along_z(halves, at[1]))
     gathered = spread(amplitudes, "ints", X_GROUPS)
     gathered, *rows = lax.optimization_barrier((gathered, *rows))
@@ -217,7 +219,6 @@
     mine = along_y(second)
     own = [gathered, swap(gathered)]
 
-    fock_rows = lax.dynamic_slice_in_dim(fock_vv, ints * amplitudes.shape[2], amplitudes.shape[2], 0)
     fock_part = fock_terms(at, fock_vv, fock_rows, [amplitudes, *own])
     rows = amplitudes.shape[1]
     sent = []

time: 67.3 us -> 66.2 us (0.984)
  Pallas kernels: 13.8 us -> 9.55 us
  waiting for transfers between devices: 23.4 us -> 26.7 us
    ppermute x6, waiting for transfers between devices: 8.58 us -> 12.3 us  [along_y(): return [row] + [lax.ppermute(row, 'amp', Y_RING(-e)) for e in (1, 2, 3)]]
    pallas_call x3, Pallas kernels: 8.03 us -> 4.85 us  [cycle_sum(): pl.pallas_call(functools.partial(cycle_kernel, first), out_shape=jax.Shap...]
    pallas_call x1, Pallas kernels: 4 us -> 2.95 us  [fock_terms(): pl.pallas_call(fock_kernel, out_shape=jax.ShapeDtypeStruct((pairs, width,...]
    all_to_all x1, waiting for transfers between devices: 2.21 us -> 1.23 us  [spread(): return lax.all_to_all(a, axis, 0, 0, axis_index_groups=groups)]
  transfers between devices with their start and end apart: 14 -> 14, of which waited for: 7 -> 8; matrix products, arithmetic and copies ran while one was open for 2% -> 2% of each run, Pallas kernels for 19% -> 13%
where the time goes in v5:
time: 66.2 us; the launch traced here: 65.9 us
  waiting for transfers between devices  26.7 us (40%)
  starting transfers between devices  25.7 us (39%)
  Pallas kernels  9.55 us (14%)
  local copies, waits for them, and re-layouts  3.67 us (6%)
    ppermute x6, waiting for transfers between devices, along_y(): return [row] + [lax.ppermute(row, 'amp', Y_RING(-e)) for e in (1, 2, 3)]  12.3 us
    ppermute x3, starting transfers between devices, along_z(): lax.ppermute(pair, 'amp', Z_RING(-2 * g))  10.2 us
    ppermute x3, waiting for transfers between devices, along_z(): lax.ppermute(pair, 'amp', Z_RING(-2 * g))  8.39 us
    ppermute x6, starting transfers between devices, along_y(): return [row] + [lax.ppermute(row, 'amp', Y_RING(-e)) for e in (1, 2, 3)]  6.84 us
    pallas_call x3, Pallas kernels, cycle_sum(): pl.pallas_call(functools.partial(cycle_kernel, first), out_shape=jax.Shap...  4.85 us
    all_to_all x1, starting transfers between devices, spread(): return lax.all_to_all(a, axis, 0, 0, axis_index_groups=groups)  4.42 us
    pallas_call x1, Pallas kernels, fock_terms(): pl.pallas_call(fock_kernel, out_shape=jax.ShapeDtypeStruct((pairs, width,...  2.95 us
    broadcast_in_dim x1, local copies, waits for them, and re-layouts, spread(): a = jnp.broadcast_to(a[None], (len(groups[0]),) + a.shape)  2.65 us
  transfers between devices with their start and end apart: 14, of which 8 were waited for; matrix products, arithmetic and copies ran while one was open for 2% of the time, Pallas kernels for 13%

profile of v5, /device:TPU:8, one launch (start us, length us, event | category | flops | bytes accessed | tf_op | source)
XLA Modules:
  0.0 65.9 jit_solution(9962181939097320573)
XLA Ops:
  0.0 2.6 %broadcast_in_dim.2 = bf16[4,2,1024,128]{3,2,1,0:T(8,128)(2,1)} broadcast(bf16[2,1024,128]{2,1,0:T(8,128)(2,1)} %refs_0_.1), dimensions={1,2,3} | broadcast | bytes 2621440 | tf_op jit(solution)/shard_map/broadcast_in_dim | solution.py:200
  2.7 4.4 %all-to-all-start = ((bf16[4,2,1024,128]{3,2,1,0:T(8,128)(2,1)}), bf16[4,2,1024,128]{3,2,1,0:T(8,128)(2,1)S(1)}, u32[]{:S(2)}, u32[]{:S(2)}) async-start(bf16[4,2,1024,128]{3,2,1,0:T(8,128)(2,1)} %broadcast_in_dim.2), calls=%async_computation | async-start | bytes 4194304 | tf_op jit(solution)/shard_map/all_to_all | solution.py:201
  7.1 1.0 %constant_dynamic-slice_fusion.rows_ref = bf16[128,1024]{1,0:T(8,128)(2,1)S(1)} fusion(bf16[1024,1024]{1,0:T(8,128)(2,1)} %fock_ref.1, s32[]{:T(128)S(6)} %select_n.43), kind=kLoop, calls=%fused_computation.23 | loop fusion | bytes 524292 | tf_op jit(solution)/shard_map/dynamic_slice | solution.py:211
  8.0 0.1 pad_add_fusion.at_ref
  8.1 0.9 %shard_map.46 = bf16[2,2,2,32,256]{4,3,2,1,0:T(8,128)(2,1)S(1)} custom-call(s32[4]{0:T(128)S(1)} %pad_add_fusion.at_ref, s32[16,16]{1,0:T(8,128)S(1)} %copy-done.3, bf16[4,32,4,128]{3,2,1,0:T(4,128)(2,1)S(1)} %copy-done.2), custom_call_target="tpu_custom_call" | custom-call | tf_op jit(solution)/shard_map/pallas_call | solution.py:170
  9.0 2.0 %collective-permute-start = (bf16[2,2,32,256]{3,2,1,0:T(8,128)(2,1)S(1)}, bf16[2,2,32,256]{3,2,1,0:T(8,128)(2,1)S(1)}, u32[]{:S(2)}, u32[]{:S(2)}) collective-permute-start(bf16[2,2,32,256]{3,2,1,0:T(8,128)(2,1)S(1)} %slice_bitcast_fusion.6), channel_id=1, source_target_pairs={{0,8},{8,0},{16,24},{24,16},{32,40},{40,32},{48,56},{56,48},{64,72... | collective-permute-start | bytes 196616 | tf_op jit(solution)/shard_map/ppermute | solution.py:188
  11.0 2.3 %collective-permute-done = bf16[2,2,32,256]{3,2,1,0:T(8,128)(2,1)S(1)} collective-permute-done((bf16[2,2,32,256]{3,2,1,0:T(8,128)(2,1)S(1)}, bf16[2,2,32,256]{3,2,1,0:T(8,128)(2,1)S(1)}, u32[]{:S(2)}, u32[]{:S(2)}) %collective-permute-start) | collective-permute-done | bytes 65568 | tf_op jit(solution)/shard_map/ppermute | solution.py:188
  13.4 7.3 %collective-permute-start.2 = (bf16[2,2,2,32,256]{4,3,2,1,0:T(8,128)(2,1)S(1)}, bf16[2,2,2,32,256]{4,3,2,1,0:T(8,128)(2,1)S(1)}, u32[]{:S(2)}, u32[]{:S(2)}) collective-permute-start(bf16[2,2,2,32,256]{4,3,2,1,0:T(8,128)(2,1)S(1)} %pad_maximum_fusion.2), channel_id=1, source_target_pairs={{0,32},{8,40},{16,48},{24,56},{32,0},{40,8},{48,16},{56,24},{64,96... | collective-permute-start | bytes 393224 | tf_op jit(solution)/shard_map/ppermute | solution.py:195
  20.7 2.9 %collective-permute-start.3 = (bf16[2,2,2,32,256]{4,3,2,1,0:T(8,128)(2,1)S(1)}, bf16[2,2,2,32,256]{4,3,2,1,0:T(8,128)(2,1)S(1)}, u32[]{:S(2)}, u32[]{:S(2)}) collective-permute-start(bf16[2,2,2,32,256]{4,3,2,1,0:T(8,128)(2,1)S(1)} %pad_maximum_fusion.2), channel_id=1, source_target_pairs={{0,16},{8,24},{16,32},{24,40},{32,48},{40,56},{48,0},{56,8},{64,80... | collective-permute-start | bytes 393224 | tf_op jit(solution)/shard_map/ppermute | solution.py:195
  23.7 2.8 %collective-permute-done.2 = bf16[2,2,2,32,256]{4,3,2,1,0:T(8,128)(2,1)S(1)} collective-permute-done((bf16[2,2,2,32,256]{4,3,2,1,0:T(8,128)(2,1)S(1)}, bf16[2,2,2,32,256]{4,3,2,1,0:T(8,128)(2,1)S(1)}, u32[]{:S(2)}, u32[]{:S(2)}) %collective-permute-start.2) | collective-permute-done | bytes 131104 | tf_op jit(solution)/shard_map/ppermute | solution.py:195
  26.4 5.6 %collective-permute-done.1 = bf16[2,2,2,32,256]{4,3,2,1,0:T(8,128)(2,1)S(1)} collective-permute-done((bf16[2,2,2,32,256]{4,3,2,1,0:T(8,128)(2,1)S(1)}, bf16[2,2,2,32,256]{4,3,2,1,0:T(8,128)(2,1)S(1)}, u32[]{:S(2)}, u32[]{:S(2)}) %collective-permute-start.1) | collective-permute-done | bytes 131104 | tf_op jit(solution)/shard_map/ppermute | solution.py:195
  32.1 0.0 collective-permute-done.3
  32.1 0.1 pad_maximum_fusion
  32.2 1.2 %all-to-all-done.refs_1_.refs_0_ = bf16[4,2,1024,128]{3,2,1,0:T(8,128)(2,1)S(1)} async-done(((bf16[4,2,1024,128]{3,2,1,0:T(8,128)(2,1)}), bf16[4,2,1024,128]{3,2,1,0:T(8,128)(2,1)S(1)}, u32[]{:S(2)}, u32[]{:S(2)}) %all-to-all-start) | async-done | bytes 2097184 | tf_op jit(solution)/shard_map/all_to_all | solution.py:201
  33.4 0.0 collective-permute-start.4
  33.4 2.3 %collective-permute-start.5 = (bf16[8,2,32,256]{3,2,1,0:T(8,128)(2,1)S(1)}, bf16[8,2,32,256]{3,2,1,0:T(8,128)(2,1)S(1)}, u32[]{:S(2)}, u32[]{:S(2)}) collective-permute-start(bf16[8,2,32,256]{3,2,1,0:T(8,128)(2,1)S(1)} %get-tuple-element.16.refs_2_), channel_id=1, source_target_pairs={{0,128},{8,136},{16,144},{24,152},{32,160},{40,168},{48,176},{56,1... | collective-permute-start | bytes 786440 | tf_op jit(solution)/shard_map/ppermute | solution.py:205
  35.7 2.0 %collective-permute-start.9 = (bf16[8,2,32,256]{3,2,1,0:T(8,128)(2,1)S(1)}, bf16[8,2,32,256]{3,2,1,0:T(8,128)(2,1)S(1)}, u32[]{:S(2)}, u32[]{:S(2)}) collective-permute-start(bf16[8,2,32,256]{3,2,1,0:T(8,128)(2,1)S(1)} %get-tuple-element.16.refs_2_), channel_id=1, source_target_pairs={{0,192},{8,200},{16,208},{24,216},{32,224},{40,232},{48,240},{56,2... | collective-permute-start | bytes 786440 | tf_op jit(solution)/shard_map/ppermute | solution.py:205
  37.7 6.3 %collective-permute-done.5.refs_4_ = bf16[8,2,32,256]{3,2,1,0:T(8,128)(2,1)S(1)} collective-permute-done((bf16[8,2,32,256]{3,2,1,0:T(8,128)(2,1)S(1)}, bf16[8,2,32,256]{3,2,1,0:T(8,128)(2,1)S(1)}, u32[]{:S(2)}, u32[]{:S(2)}) %collective-permute-start.5) | collective-permute-done | bytes 262176 | tf_op jit(solution)/shard_map/ppermute | solution.py:205
  44.1 1.6 %collective-permute-start.8 = (bf16[8,2,32,256]{3,2,1,0:T(8,128)(2,1)S(1)}, bf16[8,2,32,256]{3,2,1,0:T(8,128)(2,1)S(1)}, u32[]{:S(2)}, u32[]{:S(2)}) collective-permute-start(bf16[8,2,32,256]{3,2,1,0:T(8,128)(2,1)S(1)} %get-tuple-element.18.refs_2_), channel_id=1, source_target_pairs={{0,64},{8,72},{16,80},{24,88},{32,96},{40,104},{48,112},{56,120},{... | collective-permute-start | bytes 786440 | tf_op jit(solution)/shard_map/ppermute | solution.py:205
  45.6 0.9 %collective-permute-start.7 = (bf16[8,2,32,256]{3,2,1,0:T(8,128)(2,1)S(1)}, bf16[8,2,32,256]{3,2,1,0:T(8,128)(2,1)S(1)}, u32[]{:S(2)}, u32[]{:S(2)}) collective-permute-start(bf16[8,2,32,256]{3,2,1,0:T(8,128)(2,1)S(1)} %get-tuple-element.18.refs_2_), channel_id=1, source_target_pairs={{0,128},{8,136},{16,144},{24,152},{32,160},{40,168},{48,176},{56,1... | collective-permute-start | bytes 786440 | tf_op jit(solution)/shard_map/ppermute | solution.py:205
  46.6 3.2 %collective-permute-done.10.refs_5_ = bf16[8,2,32,256]{3,2,1,0:T(8,128)(2,1)S(1)} collective-permute-done((bf16[8,2,32,256]{3,2,1,0:T(8,128)(2,1)S(1)}, bf16[8,2,32,256]{3,2,1,0:T(8,128)(2,1)S(1)}, u32[]{:S(2)}, u32[]{:S(2)}) %collective-permute-start.10) | collective-permute-done | bytes 262176 | tf_op jit(solution)/shard_map/ppermute | solution.py:205
  49.8 1.4 %shard_map.49 = bf16[2,512,128]{2,1,0:T(8,128)(2,1)S(1)} custom-call(s32[4]{0:T(128)S(1)} %pad_add_fusion.at_ref, bf16[4,2,1024,128]{3,2,1,0:T(8,128)(2,1)S(1)} %all-to-all-done.refs_1_.refs_0_, bf16[4,2,1024,128]{3,2,1,0:T(8,128)(2,1)S(1)} %collective-permute-done.4.refs_2_.refs_1_, bf16[8,2,32,256]{3,2,1,0:T(8,128)(2,1)S(1)} %get-tuple-element.16.refs_2_, ...), custom_call_target="tpu_custom_call" | custom-call | flops 8589934592 | bytes 6291456 | tf_op jit(solution)/shard_map/pallas_call | solution.py:108
  51.2 0.0 copy-start
  51.2 0.0 copy-start.1
  51.2 2.0 %collective-permute-start.11 = (bf16[2,512,128]{2,1,0:T(8,128)(2,1)S(1)}, bf16[2,512,128]{2,1,0:T(8,128)(2,1)S(1)}, u32[]{:S(2)}, u32[]{:S(2)}) collective-permute-start(bf16[2,512,128]{2,1,0:T(8,128)(2,1)S(1)} %shard_map.49), channel_id=1, source_target_pairs={{0,8},{8,0},{16,24},{24,16},{32,40},{40,32},{48,56},{56,48},{64,72... | collective-permute-start | bytes 786440 | tf_op jit(solution)/shard_map/ppermute | solution.py:227
  53.2 1.4 %shard_map.50 = bf16[2,512,128]{2,1,0:T(8,128)(2,1)S(1)} custom-call(s32[4]{0:T(128)S(1)} %pad_add_fusion.at_ref, bf16[4,2,1024,128]{3,2,1,0:T(8,128)(2,1)S(1)} %all-to-all-done.refs_1_.refs_0_, bf16[4,2,1024,128]{3,2,1,0:T(8,128)(2,1)S(1)} %collective-permute-done.4.refs_2_.refs_1_, bf16[8,2,32,256]{3,2,1,0:T(8,128)(2,1)S(1)} %get-tuple-element.16.refs_2_, ...), custom_call_target="tpu_custom_call" | custom-call | flops 8589934592 | bytes 6291456 | tf_op jit(solution)/shard_map/pallas_call | solution.py:108
  54.6 0.2 collective-permute-start.12
  54.8 2.9 %shard_map.47.fock_ref = f32[2,1024,128]{2,1,0:T(8,128)S(1)} custom-call(s32[4]{0:T(128)S(1)} %pad_add_fusion.at_ref, bf16[1024,1024]{1,0:T(8,128)(2,1)S(1)} %copy-done, bf16[128,1024]{1,0:T(8,128)(2,1)S(1)} %constant_dynamic-slice_fusion.rows_ref, bf16[2,1024,128]{2,1,0:T(8,128)(2,1)S(1)} %copy-done.1, ...), custom_call_target="tpu_custom_call" | custom-call | flops 1073741824 | bytes 4194304 | tf_op jit(solution)/shard_map/pallas_call | solution.py:64
  57.7 2.8 %collective-permute-done.6.refs_3_ = bf16[8,2,32,256]{3,2,1,0:T(8,128)(2,1)S(1)} collective-permute-done((bf16[8,2,32,256]{3,2,1,0:T(8,128)(2,1)S(1)}, bf16[8,2,32,256]{3,2,1,0:T(8,128)(2,1)S(1)}, u32[]{:S(2)}, u32[]{:S(2)}) %collective-permute-start.6) | collective-permute-done | bytes 262176 | tf_op jit(solution)/shard_map/ppermute | solution.py:205
  60.5 2.1 %shard_map.48.mine_ref = f32[2,1024,128]{2,1,0:T(8,128)S(1)} custom-call(s32[4]{0:T(128)S(1)} %pad_add_fusion.at_ref, bf16[4,2,1024,128]{3,2,1,0:T(8,128)(2,1)S(1)} %all-to-all-done.refs_1_.refs_0_, bf16[4,2,1024,128]{3,2,1,0:T(8,128)(2,1)S(1)} %collective-permute-done.4.refs_2_.refs_1_, bf16[8,2,32,256]{3,2,1,0:T(8,128)(2,1)S(1)} %get-tuple-element.18.refs_2_, ...), custom_call_target="tpu_custom_call" | custom-call | flops 34359738368 | bytes 6291456 | tf_op jit(solution)/shard_map/pallas_call | solution.py:108
  62.7 2.4 %collective-permute-done.12.high_ref = bf16[2,512,128]{2,1,0:T(8,128)(2,1)S(1)} collective-permute-done((bf16[2,512,128]{2,1,0:T(8,128)(2,1)S(1)}, bf16[2,512,128]{2,1,0:T(8,128)(2,1)S(1)}, u32[]{:S(2)}, u32[]{:S(2)}) %collective-permute-start.12) | collective-permute-done | bytes 262176 | tf_op jit(solution)/shard_map/ppermute | solution.py:227
  65.1 0.9 %shard_map.51 = bf16[2,1024,128]{2,1,0:T(8,128)(2,1)} custom-call(f32[2,1024,128]{2,1,0:T(8,128)S(1)} %shard_map.47.fock_ref, f32[2,1024,128]{2,1,0:T(8,128)S(1)} %shard_map.48.mine_ref, bf16[2,512,128]{2,1,0:T(8,128)(2,1)S(1)} %collective-permute-done.11.low_ref, bf16[2,512,128]{2,1,0:T(8,128)(2,1)S(1)} %collective-permute-done.12.high_ref), custom_call_target="tpu_custom_call" | custom-call | tf_op jit(solution)/shard_map/pallas_call | solution.py:139
  (21 shorter events, 0.1 us)
Async XLA Ops:
  2.7 5.5 %copy-start.2 = (bf16[4,32,4,128]{3,2,1,0:T(4,128)(2,1)S(1)}, bf16[4,32,4,128]{3,2,1,0:T(4,128)(2,1)}, u32[]{:S(2)}) copy-start(bf16[4,32,4,128]{3,2,1,0:T(4,128)(2,1)} %ints_ref.1) | copy-start | bytes 393220
  2.7 5.5 %copy-start.3 = (s32[16,16]{1,0:T(8,128)S(1)}, s32[16,16]{1,0:T(8,128)}, u32[]{:S(2)}) copy-start(s32[16,16]{1,0:T(8,128)} %mask_ref.1) | copy-start | bytes 3076
  2.7 30.8 %all-to-all-start = ((bf16[4,2,1024,128]{3,2,1,0:T(8,128)(2,1)}), bf16[4,2,1024,128]{3,2,1,0:T(8,128)(2,1)S(1)}, u32[]{:S(2)}, u32[]{:S(2)}) async-start(bf16[4,2,1024,128]{3,2,1,0:T(8,128)(2,1)} %broadcast_in_dim.2), calls=%async_computation | async-start | bytes 4194304 | tf_op jit(solution)/shard_map/all_to_all | solution.py:201
  9.0 4.4 %collective-permute-start = (bf16[2,2,32,256]{3,2,1,0:T(8,128)(2,1)S(1)}, bf16[2,2,32,256]{3,2,1,0:T(8,128)(2,1)S(1)}, u32[]{:S(2)}, u32[]{:S(2)}) collective-permute-start(bf16[2,2,32,256]{3,2,1,0:T(8,128)(2,1)S(1)} %slice_bitcast_fusion.6), channel_id=1, source_target_pairs={{0,8},{8,0},{16,24},{24,16},{32,40},{40,32},{48,56},{56,48},{64,72... | collective-permute-start | bytes 196616 | tf_op jit(solution)/shard_map/ppermute | solution.py:188
  13.4 13.0 %collective-permute-start.2 = (bf16[2,2,2,32,256]{4,3,2,1,0:T(8,128)(2,1)S(1)}, bf16[2,2,2,32,256]{4,3,2,1,0:T(8,128)(2,1)S(1)}, u32[]{:S(2)}, u32[]{:S(2)}) collective-permute-start(bf16[2,2,2,32,256]{4,3,2,1,0:T(8,128)(2,1)S(1)} %pad_maximum_fusion.2), channel_id=1, source_target_pairs={{0,32},{8,40},{16,48},{24,56},{32,0},{40,8},{48,16},{56,24},{64,96... | collective-permute-start | bytes 393224 | tf_op jit(solution)/shard_map/ppermute | solution.py:195
  20.7 11.3 %collective-permute-start.1 = (bf16[2,2,2,32,256]{4,3,2,1,0:T(8,128)(2,1)S(1)}, bf16[2,2,2,32,256]{4,3,2,1,0:T(8,128)(2,1)S(1)}, u32[]{:S(2)}, u32[]{:S(2)}) collective-permute-start(bf16[2,2,2,32,256]{4,3,2,1,0:T(8,128)(2,1)S(1)} %pad_maximum_fusion.2), channel_id=1, source_target_pairs={{0,48},{8,56},{16,0},{24,8},{32,16},{40,24},{48,32},{56,40},{64,11... | collective-permute-start | bytes 393224 | tf_op jit(solution)/shard_map/ppermute | solution.py:195
  20.7 11.4 %collective-permute-start.3 = (bf16[2,2,2,32,256]{4,3,2,1,0:T(8,128)(2,1)S(1)}, bf16[2,2,2,32,256]{4,3,2,1,0:T(8,128)(2,1)S(1)}, u32[]{:S(2)}, u32[]{:S(2)}) collective-permute-start(bf16[2,2,2,32,256]{4,3,2,1,0:T(8,128)(2,1)S(1)} %pad_maximum_fusion.2), channel_id=1, source_target_pairs={{0,16},{8,24},{16,32},{24,40},{32,48},{40,56},{48,0},{56,8},{64,80... | collective-permute-start | bytes 393224 | tf_op jit(solution)/shard_map/ppermute | solution.py:195
  33.4 16.4 %collective-permute-start.4 = (bf16[4,2,1024,128]{3,2,1,0:T(8,128)(2,1)S(1)}, bf16[4,2,1024,128]{3,2,1,0:T(8,128)(2,1)S(1)}, u32[]{:S(2)}, u32[]{:S(2)}) collective-permute-start(bf16[4,2,1024,128]{3,2,1,0:T(8,128)(2,1)S(1)} %all-to-all-done.refs_1_.refs_0_), channel_id=1, source_target_pairs={{0,1},{1,0},{2,3},{3,2},{4,5},{5,4},{6,7},{7,6},{8,9},{9,8},{10,11... | collective-permute-start | bytes 6291464 | tf_op jit(solution)/shard_map/ppermute | solution.py:184
  33.4 10.7 %collective-permute-start.5 = (bf16[8,2,32,256]{3,2,1,0:T(8,128)(2,1)S(1)}, bf16[8,2,32,256]{3,2,1,0:T(8,128)(2,1)S(1)}, u32[]{:S(2)}, u32[]{:S(2)}) collective-permute-start(bf16[8,2,32,256]{3,2,1,0:T(8,128)(2,1)S(1)} %get-tuple-element.16.refs_2_), channel_id=1, source_target_pairs={{0,128},{8,136},{16,144},{24,152},{32,160},{40,168},{48,176},{56,1... | collective-permute-start | bytes 786440 | tf_op jit(solution)/shard_map/ppermute | solution.py:205
  35.7 14.1 %collective-permute-start.10 = (bf16[8,2,32,256]{3,2,1,0:T(8,128)(2,1)S(1)}, bf16[8,2,32,256]{3,2,1,0:T(8,128)(2,1)S(1)}, u32[]{:S(2)}, u32[]{:S(2)}) collective-permute-start(bf16[8,2,32,256]{3,2,1,0:T(8,128)(2,1)S(1)} %get-tuple-element.16.refs_2_), channel_id=1, source_target_pairs={{0,64},{8,72},{16,80},{24,88},{32,96},{40,104},{48,112},{56,120},{... | collective-permute-start | bytes 786440 | tf_op jit(solution)/shard_map/ppermute | solution.py:205
  35.7 14.1 %collective-permute-start.9 = (bf16[8,2,32,256]{3,2,1,0:T(8,128)(2,1)S(1)}, bf16[8,2,32,256]{3,2,1,0:T(8,128)(2,1)S(1)}, u32[]{:S(2)}, u32[]{:S(2)}) collective-permute-start(bf16[8,2,32,256]{3,2,1,0:T(8,128)(2,1)S(1)} %get-tuple-element.16.refs_2_), channel_id=1, source_target_pairs={{0,192},{8,200},{16,208},{24,216},{32,224},{40,232},{48,240},{56,2... | collective-permute-start | bytes 786440 | tf_op jit(solution)/shard_map/ppermute | solution.py:205
  44.1 13.7 %collective-permute-start.8 = (bf16[8,2,32,256]{3,2,1,0:T(8,128)(2,1)S(1)}, bf16[8,2,32,256]{3,2,1,0:T(8,128)(2,1)S(1)}, u32[]{:S(2)}, u32[]{:S(2)}) collective-permute-start(bf16[8,2,32,256]{3,2,1,0:T(8,128)(2,1)S(1)} %get-tuple-element.18.refs_2_), channel_id=1, source_target_pairs={{0,64},{8,72},{16,80},{24,88},{32,96},{40,104},{48,112},{56,120},{... | collective-permute-start | bytes 786440 | tf_op jit(solution)/shard_map/ppermute | solution.py:205
  45.6 12.1 %collective-permute-start.7 = (bf16[8,2,32,256]{3,2,1,0:T(8,128)(2,1)S(1)}, bf16[8,2,32,256]{3,2,1,0:T(8,128)(2,1)S(1)}, u32[]{:S(2)}, u32[]{:S(2)}) collective-permute-start(bf16[8,2,32,256]{3,2,1,0:T(8,128)(2,1)S(1)} %get-tuple-element.18.refs_2_), channel_id=1, source_target_pairs={{0,128},{8,136},{16,144},{24,152},{32,160},{40,168},{48,176},{56,1... | collective-permute-start | bytes 786440 | tf_op jit(solution)/shard_map/ppermute | solution.py:205
  49.8 10.7 %collective-permute-start.6 = (bf16[8,2,32,256]{3,2,1,0:T(8,128)(2,1)S(1)}, bf16[8,2,32,256]{3,2,1,0:T(8,128)(2,1)S(1)}, u32[]{:S(2)}, u32[]{:S(2)}) collective-permute-start(bf16[8,2,32,256]{3,2,1,0:T(8,128)(2,1)S(1)} %get-tuple-element.18.refs_2_), channel_id=1, source_target_pairs={{0,192},{8,200},{16,208},{24,216},{32,224},{40,232},{48,240},{56,2... | collective-permute-start | bytes 786440 | tf_op jit(solution)/shard_map/ppermute | solution.py:205
  51.2 3.6 %copy-start = (bf16[1024,1024]{1,0:T(8,128)(2,1)S(1)}, bf16[1024,1024]{1,0:T(8,128)(2,1)}, u32[]{:S(2)}) copy-start(bf16[1024,1024]{1,0:T(8,128)(2,1)} %fock_ref.1) | copy-start | bytes 6291460
  51.2 3.6 %copy-start.1 = (bf16[2,1024,128]{2,1,0:T(8,128)(2,1)S(1)}, bf16[2,1024,128]{2,1,0:T(8,128)(2,1)}, u32[]{:S(2)}) copy-start(bf16[2,1024,128]{2,1,0:T(8,128)(2,1)} %refs_0_.1) | copy-start | bytes 1572868
  51.2 11.5 %collective-permute-start.11 = (bf16[2,512,128]{2,1,0:T(8,128)(2,1)S(1)}, bf16[2,512,128]{2,1,0:T(8,128)(2,1)S(1)}, u32[]{:S(2)}, u32[]{:S(2)}) collective-permute-start(bf16[2,512,128]{2,1,0:T(8,128)(2,1)S(1)} %shard_map.49), channel_id=1, source_target_pairs={{0,8},{8,0},{16,24},{24,16},{32,40},{40,32},{48,56},{56,48},{64,72... | collective-permute-start | bytes 786440 | tf_op jit(solution)/shard_map/ppermute | solution.py:227
  54.6 10.5 %collective-permute-start.12 = (bf16[2,512,128]{2,1,0:T(8,128)(2,1)S(1)}, bf16[2,512,128]{2,1,0:T(8,128)(2,1)S(1)}, u32[]{:S(2)}, u32[]{:S(2)}) collective-permute-start(bf16[2,512,128]{2,1,0:T(8,128)(2,1)S(1)} %shard_map.50), channel_id=1, source_target_pairs={{0,8},{8,0},{16,24},{24,16},{32,40},{40,32},{48,56},{56,48},{64,72... | collective-permute-start | bytes 786440 | tf_op jit(solution)/shard_map/ppermute | solution.py:227
